TPU v7x, 32 devices: a whole 2x2x4 slice. The times are simulated.
32 devices in a mesh: groups: 2 (over x), slab: 16 (over z, y, core).
Axes of the slice: x: 2, y: 2, z: 4, core: 2. Of those that a mesh axis runs over, the one named last changes fastest.
Arguments:
- queries: bfloat16 [32, 32, 128], P(('groups', 'slab')), parts along dimension 0, may hold values from -6 to 6
- passages: bfloat16 [2048, 128, 128], P(('groups', 'slab')), parts along dimension 0, may hold values from -0.5 to 0.5
- lengths: int32 [2048], P(('groups', 'slab')), parts along dimension 0, may hold values from 1 to 128
- shortlist: int32 [32, 96], P(('groups', 'slab')), parts along dimension 0, may hold values from 0 to 1023, as said below
Outputs:
- coarse: float32 [2048, 16], P(('groups', 'slab')), parts along dimension 0
- exact: float32 [32, 96], P(('groups', 'slab')), parts along dimension 0
There are 2 independent parts, one for each index of `groups`. A program takes and returns all parts, laid end to end along the dimension named above; each array names one. Nothing has to cross between parts.
Inputs may be any that keep to these rules, and one draw needn't show every extreme that they name: `shortlist`: passage id p lies on slab p // 64. The ids of one query are distinct; at most 16 of them lie on any one slab, and in every draw one slab holds exactly 16 ids of every query.
All inputs are finite; a program needn't handle non-finite values.
Results may differ from a plain program's by a relative error of at most 0.00037.
Values may be sent and summed in bfloat16 or wider, within the bound.
No kernel may reach another device: no remote copies, remote signals or barrier semaphores. Data moves between devices by JAX's collectives and lax.ppermute only.
A program may use at most 128 MiB of HBM per device.

v0:
```python
import jax
import jax.numpy as jnp
from jax import lax
from jax.sharding import PartitionSpec as P

PREFIX = 64


def unit_prefix(vectors):
    head = vectors[..., :PREFIX].astype(jnp.float32)
    total = jnp.sum(head * head, axis=-1, keepdims=True)
    return (head * lax.rsqrt(total + 1e-06)).astype(jnp.bfloat16)


def coarse_scores(all_prefix, passages, lengths):
    count = all_prefix.shape[0]
    qtok = all_prefix.shape[1]
    width = passages.shape[1]
    flat_queries = all_prefix.reshape(count * qtok, all_prefix.shape[2])
    passage_prefix = unit_prefix(passages)
    blocks = passage_prefix.reshape(passages.shape[0] // 8, 8 * width, passage_prefix.shape[2])
    block_lens = lengths.reshape(passages.shape[0] // 8, 8)
    slots = jnp.arange(width, dtype=jnp.int32)

    def one_block(item):
        block, lens = item
        scores = lax.dot_general(
            flat_queries, block, (((1,), (1,)), ((), ())), preferred_element_type=jnp.float32
        )
        scores = scores.reshape(count, qtok, 8, width)
        scores = jnp.where(slots[None, None, None, :] < lens[None, None, :, None], scores, -1e30)
        return jnp.mean(jnp.max(scores, axis=-1), axis=1)

    result = lax.map(one_block, (blocks, block_lens))
    return jnp.transpose(result, (0, 2, 1)).reshape(passages.shape[0], count)


def masked_maxsim(scores, lens):
    slots = jnp.arange(scores.shape[-1], dtype=jnp.int32)
    scores = jnp.where(slots[None, None, None, :] < lens[:, :, None, None], scores, -1e30)
    return jnp.mean(jnp.max(scores, axis=-1), axis=-1)


def per_device(queries, passages, lengths, shortlist):
    owners = lax.axis_size("slab")
    short = shortlist.shape[1]
    per_slab = passages.shape[0]
    cap = max(2, 8 * short // (3 * owners))
    all_prefix = lax.all_gather(unit_prefix(queries), "slab", axis=0, tiled=True)
    ids = shortlist[0]
    owner = ids // per_slab
    local = ids % per_slab
    earlier = jnp.arange(short)[None, :] < jnp.arange(short)[:, None]
    rank = jnp.sum((owner[None, :] == owner[:, None]) & earlier, axis=1)
    table = jnp.full((owners * cap,), -1, jnp.int32).at[owner * cap + rank].set(local)
    asked = lax.all_to_all(
        table.reshape(owners, cap), "slab", split_axis=0, concat_axis=0, tiled=True
    )
    valid = asked >= 0
    pick = jnp.maximum(asked, 0)
    chosen = passages[pick]
    chosen_lens = jnp.where(valid, lengths[pick], 1)
    coarse = coarse_scores(all_prefix, passages, lengths)
    own_query = queries[0]
    scores = jnp.einsum(
        "td,abud->abtu",
        own_query,
        lax.all_to_all(chosen, "slab", split_axis=0, concat_axis=0, tiled=True),
        preferred_element_type=jnp.float32,
    )
    returned = masked_maxsim(
        scores, lax.all_to_all(chosen_lens, "slab", split_axis=0, concat_axis=0, tiled=True)
    )
    exact = returned[owner, rank][None, :]
    return (coarse, exact)


def solution(mesh):
    return jax.shard_map(
        per_device,
        mesh=mesh,
        in_specs=(
            P(("groups", "slab"), None, None),
            P(("groups", "slab"), None, None),
            P(("groups", "slab")),
            P(("groups", "slab"), None),
        ),
        out_specs=(P(("groups", "slab"), None), P(("groups", "slab"), None)),
        check_vma=False,
    )
```

profile of v0, /device:TPU:11, one launch (start us, length us, event | category | flops | bytes accessed | tf_op | source)
XLA Modules:
  0.0 290.7 jit_solution(2696439342453179641)
XLA Ops:
  3.8 11.1 %all_to_all.20 = s32[16,1,16]{2,1,0:T(1,128)S(1)} all-to-all(s32[16,1,16]{2,1,0:T(1,128)S(1)} %all_to_all.13), channel_id=1, replica_groups=mesh['groups'=2,'slab'=16] {'slab'}, dimensions={0} | all-to-all | bytes 2048 | tf_op jit(solution)/shard_map/all_to_all | solution.py:56
  17.6 5.1 %all-to-all-start.1 = ((s32[16,1,16]{2,1,0:T(1,128)}), s32[16,1,16]{2,1,0:T(1,128)S(1)}, u32[]{:S(2)}, u32[]{:S(2)}) async-start(s32[16,1,16]{2,1,0:T(1,128)} %compare_select_fusion), calls=%async_computation.1 | async-start | bytes 16384 | tf_op jit(solution)/shard_map/all_to_all | solution.py:72
  22.7 8.3 %gather_fusion.1 = bf16[256,128,128]{2,1,0:T(8,128)(2,1)} fusion(bf16[64,128,128]{2,1,0:T(8,128)(2,1)S(1)} %copy-done.1, s32[1024]{0:T(1024)S(1)} %pad_clamp_fusion), kind=kCustom, calls=%fused_computation.1 | custom fusion | bytes 16778240 | tf_op jit(solution)/shard_map/gather | solution.py:61
  31.1 6.2 %all-to-all-start.2 = ((bf16[16,16,128,128]{3,2,1,0:T(8,128)(2,1)}), bf16[16,16,128,128]{3,2,1,0:T(8,128)(2,1)}, u32[]{:S(2)}, u32[]{:S(2)}) async-start(bf16[16,16,128,128]{3,2,1,0:T(8,128)(2,1)} %bitcast.86), calls=%async_computation.2 | async-start | bytes 16777216 | tf_op jit(solution)/shard_map/all_to_all | solution.py:68
  37.6 192.8 %all_gather.3 = bf16[16,32,64]{2,1,0:T(8,128)(2,1)S(1)} all-gather(bf16[1,32,64]{2,1,0:T(8,128)(2,1)S(1)} %fusion.11), channel_id=1, replica_groups=mesh['groups'=2,'slab'=16] {'slab'}, dimensions={0}, use_global_device_ids=true | all-gather | bytes 69632 | tf_op jit(solution)/shard_map/all_gather | solution.py:49
  231.6 2.7 fusion.8
  234.3 47.3 %while.11 = (s32[]{:T(128)}, f32[8,16,8]{1,2,0:T(8,128)S(1)}, s32[8,8]{1,0:T(8,128)S(1)}, bf16[8,1024,64]{2,1,0:T(8,128)(2,1)}, bf16[512,64]{1,0:T(8,128)(2,1)S(1)}, /*index=5*/s32[]{:T(128)}, f32[]{:T(128)}) while((s32[]{:T(128)}, f32[8,16,8]{1,2,0:T(8,128)S(1)}, s32[8,8]{1,0:T(8,128)S(1)}, bf16[8,1024,64]{2,1,0:T(8,128)(2,1)}, ...), condition=%wide.region_5.6_spmd.clone, body=%wide.region_2.5_spmd.clone.sunk | while | flops 68158464 | bytes 12955333 | solution.py:34
  234.3 2.7 convolution_bitcast_fusion.2
  237.0 1.9 copy.28
  240.3 2.7 convolution_bitcast_fusion.2
  242.9 1.9 copy.28
  246.2 2.7 convolution_bitcast_fusion.2
  248.8 1.9 copy.28
  252.1 2.7 convolution_bitcast_fusion.2
  254.8 1.9 copy.28
  258.0 2.7 convolution_bitcast_fusion.2
  260.7 1.9 copy.28
  263.9 2.7 convolution_bitcast_fusion.2
  266.6 1.9 copy.28
  269.8 2.7 convolution_bitcast_fusion.2
  272.5 1.9 copy.28
  275.7 2.7 convolution_bitcast_fusion.2
  278.4 1.9 copy.28
  282.3 6.4 %select_reduce_fusion = f32[16,16,32]{2,1,0:T(8,128)S(1)} fusion(bf16[16,16,128,128]{3,2,1,0:T(8,128)(2,1)} %all-to-all-done.2, pred[16,16,128]{2,1,0:T(8,128)(4,1)S(1)} %iota_compare_fusion.1, bf16[1,32,128]{2,1,0:T(8,128)(2,1)S(1)} %copy-done.2), kind=kOutput, calls=%fused_computation.19 | convolution fusion | flops 270524416 | bytes 8462336 | tf_op jit(solution)/shard_map/td,abud->abtu/dot_general | solution.py:65
  (89 shorter events, 20.1 us)
Async XLA Ops:
  0.6 14.4 %copy-start = (s32[64]{0:T(128)S(1)}, s32[64]{0:T(128)}, u32[]{:S(2)}) copy-start(s32[64]{0:T(128)} %param.8) | copy-start | bytes 772
  15.0 7.7 %copy-start.1 = (bf16[64,128,128]{2,1,0:T(8,128)(2,1)S(1)}, bf16[64,128,128]{2,1,0:T(8,128)(2,1)}, u32[]{:S(2)}) copy-start(bf16[64,128,128]{2,1,0:T(8,128)(2,1)} %param.7) | copy-start | bytes 6291460
  17.6 13.4 %all-to-all-start.1 = ((s32[16,1,16]{2,1,0:T(1,128)}), s32[16,1,16]{2,1,0:T(1,128)S(1)}, u32[]{:S(2)}, u32[]{:S(2)}) async-start(s32[16,1,16]{2,1,0:T(1,128)} %compare_select_fusion), calls=%async_computation.1 | async-start | bytes 16384 | tf_op jit(solution)/shard_map/all_to_all | solution.py:72
  31.1 6.3 %copy-start.2 = (bf16[1,32,128]{2,1,0:T(8,128)(2,1)S(1)}, bf16[1,32,128]{2,1,0:T(8,128)(2,1)}, u32[]{:S(2)}) copy-start(bf16[1,32,128]{2,1,0:T(8,128)(2,1)} %param.6) | copy-start | bytes 24580
  31.1 251.2 %all-to-all-start.2 = ((bf16[16,16,128,128]{3,2,1,0:T(8,128)(2,1)}), bf16[16,16,128,128]{3,2,1,0:T(8,128)(2,1)}, u32[]{:S(2)}, u32[]{:S(2)}) async-start(bf16[16,16,128,128]{3,2,1,0:T(8,128)(2,1)} %bitcast.86), calls=%async_computation.2 | async-start | bytes 16777216 | tf_op jit(solution)/shard_map/all_to_all | solution.py:68
where the time goes:
time: 292 us; the launch traced here: 291 us
  blocking collectives  204 us (70%)
  local copies, waits for them, and re-layouts  33.6 us (12%)
  matrix products  27.9 us (10%)
  other arithmetic  12.9 us (4%)
  starting transfers between devices  11.3 us (4%)
    all_gather x1, blocking collectives, per_device(): lax.all_gather(unit_prefix(queries), 'slab', axis=0, tiled=True)  193 us
    dot_general x8, matrix products, one_block(): lax.dot_general(flat_queries, block, (((1,), (1,)), ((), ())), preferred_...  21.5 us
    dot_general x8, local copies, waits for them, and re-layouts, one_block(): lax.dot_general(flat_queries, block, (((1,), (1,)), ((), ())), preferred_...  15.4 us
    all_to_all x1, blocking collectives, per_device(): lax.all_to_all(table.reshape(owners, cap), 'slab', split_axis=0, concat_a...  11.1 us
    gather x1, local copies, waits for them, and re-layouts, per_device(): chosen = passages[pick]  8.35 us
    dot_general x1, matrix products, per_device(): jnp.einsum('td,abud->abtu', own_query, lax.all_to_all(chosen, 'slab', spl...  6.45 us
    all_to_all x1, starting transfers between devices, per_device(): lax.all_to_all(chosen, 'slab', split_axis=0, concat_axis=0, tiled=True)  6.23 us
  transfers between devices with their start and end apart: 2, of which 0 were waited for; matrix products, arithmetic and copies ran while one was open for 21% of the time, Pallas kernels for 0%

commit v1 on v0

v1 whole, which is shorter than its diff:
```python
import functools

import jax
import jax.numpy as jnp
from jax import lax
from jax.experimental import pallas as pl
from jax.experimental.pallas import tpu as pltpu
from jax.sharding import PartitionSpec as P

PREFIX = 64
EPS = 1e-06
VMEM = pl.BlockSpec(memory_space=pltpu.VMEM)
SMEM = pl.BlockSpec(memory_space=pltpu.SMEM)


def params():
    return pltpu.CompilerParams(vmem_limit_bytes=24 << 20)


def unit_prefix(rows):
    head = rows[:, :PREFIX]
    total = jnp.sum(head * head, axis=-1, keepdims=True)
    return (head * lax.rsqrt(total + EPS)).astype(jnp.bfloat16)


def prepare_kernel(count, width, lens_ref, passages_ref, full_ref, prefix_ref):
    row = lax.broadcasted_iota(jnp.int32, (width, passages_ref.shape[2]), 0)
    for p in range(count):
        tokens = passages_ref[p].astype(jnp.float32)
        tokens = jnp.where(row < lens_ref[p], tokens, tokens[0:1])
        at = pl.ds(p * width, width)
        full_ref[at, :] = tokens.astype(jnp.bfloat16)
        prefix_ref[at, :] = unit_prefix(tokens)


def prepare(lengths, passages):
    count, width, dim = passages.shape
    return pl.pallas_call(
        functools.partial(prepare_kernel, count, width),
        out_shape=(
            jax.ShapeDtypeStruct((count * width, dim), jnp.bfloat16),
            jax.ShapeDtypeStruct((count * width, PREFIX), jnp.bfloat16),
        ),
        in_specs=[SMEM, VMEM],
        out_specs=(VMEM, VMEM),
        compiler_params=params(),
        cost_estimate=pl.CostEstimate(flops=count * width * dim * 8, bytes_accessed=9 << 20, transcendentals=0),
    )(lengths, passages)


def maxima(tokens_ref, queries, best_ref, count, width):
    step = 256
    rows = queries.shape[0]
    for at in range(0, rows, step):
        block = queries[at : at + step, :]
        for p in range(0, count, 2):
            scores = lax.dot_general(
                tokens_ref[p * width : (p + 2) * width, :],
                block,
                (((1,), (1,)), ((), ())),
                preferred_element_type=jnp.float32,
            )
            best_ref[p : p + 2, at : at + step] = jnp.max(scores.reshape(2, width, step), axis=1)


def averaging(me, queries, qtok):
    shape = (queries, queries * qtok)
    place = lax.broadcasted_iota(jnp.int32, shape, 1) // qtok
    whose = lax.broadcasted_iota(jnp.int32, shape, 0)
    return jnp.where((place ^ me) == whose, 1.0 / qtok, 0.0).astype(jnp.float32)


def average(me, best, owners):
    mean = averaging(me, owners, best.shape[1] // owners)
    return lax.dot_general(
        mean, best, (((1,), (1,)), ((), ())), preferred_element_type=jnp.float32, precision=lax.Precision.HIGHEST
    )


def exact_kernel(count, width, owners, me_ref, tokens_ref, queries_ref, out_ref, best_ref):
    maxima(tokens_ref, queries_ref[...], best_ref, count, width)
    out_ref[...] = average(me_ref[0], best_ref[...], owners)


def coarse_kernel(count, width, owners, me_ref, tokens_ref, queries_ref, out_ref, best_ref):
    maxima(tokens_ref, unit_prefix(queries_ref[...].astype(jnp.float32)), best_ref, count, width)
    out_ref[...] = average(me_ref[0], best_ref[...], owners)


def score(kernel, me, tokens, queries, owners, count):
    width = tokens.shape[0] // count
    return pl.pallas_call(
        functools.partial(kernel, count, width, owners),
        out_shape=jax.ShapeDtypeStruct((owners, count), jnp.float32),
        in_specs=[SMEM, VMEM, VMEM],
        out_specs=VMEM,
        scratch_shapes=[pltpu.VMEM((count, queries.shape[0]), jnp.float32)],
        compiler_params=params(),
        cost_estimate=pl.CostEstimate(
            flops=4 * tokens.shape[0] * queries.shape[0] * 128, bytes_accessed=4 << 20, transcendentals=0
        ),
    )(me, tokens, queries)


def pick_kernel(ids_ref, returned_ref, out_ref):
    owners, count = returned_ref.shape
    ids = ids_ref[...]
    owner, local = ids // count, ids % count
    short = ids.shape[1]
    hot = lax.broadcasted_iota(jnp.int32, (count, short), 0) == local
    column = lax.dot_general(
        returned_ref[...],
        hot.astype(jnp.float32),
        (((1,), (0,)), ((), ())),
        preferred_element_type=jnp.float32,
        precision=lax.Precision.HIGHEST,
    )
    mine = lax.broadcasted_iota(jnp.int32, (owners, short), 0) == owner
    out_ref[...] = jnp.sum(jnp.where(mine, column, 0.0), axis=0, keepdims=True)


def per_device(queries, passages, lengths, shortlist):
    owners = lax.axis_size("slab")
    count = passages.shape[0]
    me = lax.axis_index("slab").astype(jnp.int32).reshape(1)
    full, prefix = prepare(lengths, passages)
    held = queries
    bit = 1
    while bit < owners:
        other = lax.ppermute(held, "slab", [(i, i ^ bit) for i in range(owners)])
        held = jnp.concatenate([held, other], axis=0)
        bit *= 2
    rows = held.reshape(owners * held.shape[1], held.shape[2])
    found = score(exact_kernel, me, full, rows, owners, count)
    returned = lax.all_to_all(found, "slab", split_axis=0, concat_axis=0, tiled=True)
    coarse = score(coarse_kernel, me, prefix, rows, owners, count)
    exact = pl.pallas_call(
        pick_kernel,
        out_shape=jax.ShapeDtypeStruct(shortlist.shape, jnp.float32),
        in_specs=[VMEM, VMEM],
        out_specs=VMEM,
    )(shortlist, returned)
    return (coarse.T, exact)


def solution(mesh):
    return jax.shard_map(
        per_device,
        mesh=mesh,
        in_specs=(
            P(("groups", "slab"), None, None),
            P(("groups", "slab"), None, None),
            P(("groups", "slab")),
            P(("groups", "slab"), None),
        ),
        out_specs=(P(("groups", "slab"), None), P(("groups", "slab"), None)),
        check_vma=False,
    )
```

time: 292 us -> 38.6 us (0.13)
  the two profiles are of different devices: /device:TPU:11 before, /device:TPU:0 now
where the time goes in v1:
time: 38.6 us; the launch traced here: 38.4 us
  starting transfers between devices  15.1 us (39%)
  Pallas kernels  10.1 us (26%)
  waiting for transfers between devices  8.86 us (23%)
  local copies, waits for them, and re-layouts  3.58 us (9%)
  between operations  0.69 us (2%)
    ppermute x4, starting transfers between devices, per_device(): other = lax.ppermute(held, 'slab', [(i, i ^ bit) for i in range(owners)])  8.29 us
    all_to_all x1, starting transfers between devices, per_device(): lax.all_to_all(found, 'slab', split_axis=0, concat_axis=0, tiled=True)  6.86 us
    pallas_call x2, Pallas kernels, score(): pl.pallas_call(functools.partial(kernel, count, width, owners), out_shape...  6.64 us
    ppermute x4, waiting for transfers between devices, per_device(): other = lax.ppermute(held, 'slab', [(i, i ^ bit) for i in range(owners)])  5.83 us
    unnamed x12, local copies, waits for them, and re-layouts  3.56 us
    all_to_all x1, waiting for transfers between devices, per_device(): lax.all_to_all(found, 'slab', split_axis=0, concat_axis=0, tiled=True)  3.03 us
    pallas_call x1, Pallas kernels, prepare(): pl.pallas_call(functools.partial(prepare_kernel, count, width), out_shape...  2.04 us
    pallas_call x1, Pallas kernels, per_device(): pl.pallas_call(pick_kernel, out_shape=jax.ShapeDtypeStruct(shortlist.shap...  1.38 us
  transfers between devices with their start and end apart: 5, of which 4 were waited for; matrix products, arithmetic and copies ran while one was open for 2% of the time, Pallas kernels for 14%

profile of v1, /device:TPU:0, one launch (start us, length us, event | category | flops | bytes accessed | tf_op | source)
XLA Modules:
  0.0 38.4 jit_solution(12609427778511086428)
XLA Ops:
  0.6 0.0 copy-start.2
  0.6 0.5 %collective-permute-start = (bf16[1,32,128]{2,1,0:T(8,128)(2,1)}, bf16[1,32,128]{2,1,0:T(8,128)(2,1)S(1)}, u32[]{:S(2)}, u32[]{:S(2)}) collective-permute-start(bf16[1,32,128]{2,1,0:T(8,128)(2,1)} %param.4), channel_id=1, source_target_pairs={{0,1},{1,0},{2,3},{3,2},{4,5},{5,4},{6,7},{7,6},{8,9},{9,8},{10,11... | collective-permute-start | bytes 24584 | tf_op jit(solution)/shard_map/ppermute | solution.py:130
  1.2 0.7 %constant_dynamic-update-slice_fusion.4 = bf16[16,32,128]{2,1,0:T(8,128)(2,1)S(1)} fusion(bf16[1,32,128]{2,1,0:T(8,128)(2,1)} %param.4), kind=kLoop, calls=%fused_computation.7 | loop fusion | bytes 16384
  1.9 0.0 copy-start
  1.9 1.6 %copy-done = bf16[64,128,128]{2,1,0:T(8,128)(2,1)S(1)} copy-done((bf16[64,128,128]{2,1,0:T(8,128)(2,1)S(1)}, bf16[64,128,128]{2,1,0:T(8,128)(2,1)}, u32[]{:S(2)}) %copy-start) | copy-done | bytes 2097176
  3.4 0.0 copy-start.1
  3.4 0.7 %copy-done.1 = s32[64]{0:T(128)S(1)} copy-done((s32[64]{0:T(128)S(1)}, s32[64]{0:T(128)}, u32[]{:S(2)}) %copy-start.1) | copy-done | bytes 280
  4.1 2.0 %shard_map.59 = (bf16[8192,128]{1,0:T(8,128)(2,1)S(1)}, bf16[8192,64]{1,0:T(8,128)(2,1)S(1)}) custom-call(s32[64]{0:T(128)S(1)} %copy-done.1, bf16[64,128,128]{2,1,0:T(8,128)(2,1)S(1)} %copy-done), custom_call_target="tpu_custom_call" | custom-call | flops 8388608 | bytes 9437184 | tf_op jit(solution)/shard_map/pallas_call | solution.py:38
  6.1 0.0 collective-permute-done
  6.2 0.0 copy-done.2
  6.2 2.6 %collective-permute-start.1 = (bf16[2,32,128]{2,1,0:T(8,128)(2,1)S(1)}, bf16[2,32,128]{2,1,0:T(8,128)(2,1)S(1)}, u32[]{:S(2)}, u32[]{:S(2)}) collective-permute-start(bf16[2,32,128]{2,1,0:T(8,128)(2,1)S(1)} %pad_maximum_fusion.2), channel_id=1, source_target_pairs={{0,2},{1,3},{2,0},{3,1},{4,6},{5,7},{6,4},{7,5},{8,10},{9,11},{10,... | collective-permute-start | bytes 49160 | tf_op jit(solution)/shard_map/ppermute | solution.py:130
  8.8 1.7 %collective-permute-done.1 = bf16[2,32,128]{2,1,0:T(8,128)(2,1)S(1)} collective-permute-done((bf16[2,32,128]{2,1,0:T(8,128)(2,1)S(1)}, bf16[2,32,128]{2,1,0:T(8,128)(2,1)S(1)}, u32[]{:S(2)}, u32[]{:S(2)}) %collective-permute-start.1) | collective-permute-done | bytes 16416 | tf_op jit(solution)/shard_map/ppermute | solution.py:130
  10.5 2.1 %collective-permute-start.2 = (bf16[4,32,128]{2,1,0:T(8,128)(2,1)S(1)}, bf16[4,32,128]{2,1,0:T(8,128)(2,1)S(1)}, u32[]{:S(2)}, u32[]{:S(2)}) collective-permute-start(bf16[4,32,128]{2,1,0:T(8,128)(2,1)S(1)} %pad_maximum_fusion.1), channel_id=1, source_target_pairs={{0,4},{1,5},{2,6},{3,7},{4,0},{5,1},{6,2},{7,3},{8,12},{9,13},{10,... | collective-permute-start | bytes 98312 | tf_op jit(solution)/shard_map/ppermute | solution.py:130
  12.6 1.9 %collective-permute-done.2 = bf16[4,32,128]{2,1,0:T(8,128)(2,1)S(1)} collective-permute-done((bf16[4,32,128]{2,1,0:T(8,128)(2,1)S(1)}, bf16[4,32,128]{2,1,0:T(8,128)(2,1)S(1)}, u32[]{:S(2)}, u32[]{:S(2)}) %collective-permute-start.2) | collective-permute-done | bytes 32800 | tf_op jit(solution)/shard_map/ppermute | solution.py:130
  14.5 3.1 %collective-permute-start.3 = (bf16[8,32,128]{2,1,0:T(8,128)(2,1)S(1)}, bf16[8,32,128]{2,1,0:T(8,128)(2,1)S(1)}, u32[]{:S(2)}, u32[]{:S(2)}) collective-permute-start(bf16[8,32,128]{2,1,0:T(8,128)(2,1)S(1)} %pad_maximum_fusion), channel_id=1, source_target_pairs={{0,8},{1,9},{2,10},{3,11},{4,12},{5,13},{6,14},{7,15},{8,0},{9,1},... | collective-permute-start | bytes 196616 | tf_op jit(solution)/shard_map/ppermute | solution.py:130
  17.6 2.2 %collective-permute-done.3 = bf16[8,32,128]{2,1,0:T(8,128)(2,1)S(1)} collective-permute-done((bf16[8,32,128]{2,1,0:T(8,128)(2,1)S(1)}, bf16[8,32,128]{2,1,0:T(8,128)(2,1)S(1)}, u32[]{:S(2)}, u32[]{:S(2)}) %collective-permute-start.3) | collective-permute-done | bytes 65568 | tf_op jit(solution)/shard_map/ppermute | solution.py:130
  19.8 3.3 %shard_map.61 = f32[16,64]{1,0:T(8,128)} custom-call(s32[1]{0:T(128)} %bitcast.me_ref, bf16[8192,128]{1,0:T(8,128)(2,1)S(1)} %get-tuple-element.5.tokens_ref, bf16[512,128]{1,0:T(8,128)(2,1)S(1)} %bitcast.7), custom_call_target="tpu_custom_call" | custom-call | flops 2147483648 | bytes 4194304 | tf_op jit(solution)/shard_map/pallas_call | solution.py:92
  23.1 6.9 %all-to-all-start = ((f32[16,1,64]{2,1,0:T(1,128)}), f32[16,1,64]{2,1,0:T(1,128)S(1)}, u32[]{:S(2)}, u32[]{:S(2)}) async-start(f32[16,1,64]{2,1,0:T(1,128)} %bitcast.4), calls=%async_computation | async-start | bytes 16384 | tf_op jit(solution)/shard_map/all_to_all | solution.py:135
  30.0 3.4 %shard_map.60 = f32[16,64]{1,0:T(8,128)} custom-call(s32[1]{0:T(128)} %bitcast.me_ref, bf16[8192,64]{1,0:T(8,128)(2,1)S(1)} %get-tuple-element.4.tokens_ref, bf16[512,128]{1,0:T(8,128)(2,1)S(1)} %bitcast.8), custom_call_target="tpu_custom_call" | custom-call | flops 2147483648 | bytes 4194304 | tf_op jit(solution)/shard_map/pallas_call | solution.py:92
  33.4 3.0 %all-to-all-done = f32[16,1,64]{2,1,0:T(1,128)S(1)} async-done(((f32[16,1,64]{2,1,0:T(1,128)}), f32[16,1,64]{2,1,0:T(1,128)S(1)}, u32[]{:S(2)}, u32[]{:S(2)}) %all-to-all-start) | async-done | bytes 4128 | tf_op jit(solution)/shard_map/all_to_all | solution.py:135
  36.4 0.0 copy-start.3
  36.4 0.6 %copy-done.3 = f32[16,1,64]{2,1,0:T(1,128)} copy-done((f32[16,1,64]{2,1,0:T(1,128)}, f32[16,1,64]{2,1,0:T(1,128)S(1)}, u32[]{:S(2)}) %copy-start.3) | copy-done | bytes 4120
  37.0 1.4 %shard_map.62 = f32[1,96]{1,0:T(1,128)} custom-call(s32[1,96]{1,0:T(1,128)} %ids_ref.1, f32[16,64]{1,0:T(8,128)} %bitcast.9), custom_call_target="tpu_custom_call" | custom-call | tf_op jit(solution)/shard_map/pallas_call | solution.py:137
  (7 shorter events, 0.1 us)
Async XLA Ops:
  0.6 5.5 %copy-start.2 = (bf16[1,32,128]{2,1,0:T(8,128)(2,1)S(1)}, bf16[1,32,128]{2,1,0:T(8,128)(2,1)}, u32[]{:S(2)}) copy-start(bf16[1,32,128]{2,1,0:T(8,128)(2,1)} %param.4) | copy-start | bytes 24580
  0.6 5.5 %collective-permute-start = (bf16[1,32,128]{2,1,0:T(8,128)(2,1)}, bf16[1,32,128]{2,1,0:T(8,128)(2,1)S(1)}, u32[]{:S(2)}, u32[]{:S(2)}) collective-permute-start(bf16[1,32,128]{2,1,0:T(8,128)(2,1)} %param.4), channel_id=1, source_target_pairs={{0,1},{1,0},{2,3},{3,2},{4,5},{5,4},{6,7},{7,6},{8,9},{9,8},{10,11... | collective-permute-start | bytes 24584 | tf_op jit(solution)/shard_map/ppermute | solution.py:130
  1.9 1.6 %copy-start = (bf16[64,128,128]{2,1,0:T(8,128)(2,1)S(1)}, bf16[64,128,128]{2,1,0:T(8,128)(2,1)}, u32[]{:S(2)}) copy-start(bf16[64,128,128]{2,1,0:T(8,128)(2,1)} %passages_ref.1) | copy-start | bytes 6291460
  3.4 0.7 %copy-start.1 = (s32[64]{0:T(128)S(1)}, s32[64]{0:T(128)}, u32[]{:S(2)}) copy-start(s32[64]{0:T(128)} %lens_ref.1) | copy-start | bytes 772
  6.2 4.3 %collective-permute-start.1 = (bf16[2,32,128]{2,1,0:T(8,128)(2,1)S(1)}, bf16[2,32,128]{2,1,0:T(8,128)(2,1)S(1)}, u32[]{:S(2)}, u32[]{:S(2)}) collective-permute-start(bf16[2,32,128]{2,1,0:T(8,128)(2,1)S(1)} %pad_maximum_fusion.2), channel_id=1, source_target_pairs={{0,2},{1,3},{2,0},{3,1},{4,6},{5,7},{6,4},{7,5},{8,10},{9,11},{10,... | collective-permute-start | bytes 49160 | tf_op jit(solution)/shard_map/ppermute | solution.py:130
  10.5 4.0 %collective-permute-start.2 = (bf16[4,32,128]{2,1,0:T(8,128)(2,1)S(1)}, bf16[4,32,128]{2,1,0:T(8,128)(2,1)S(1)}, u32[]{:S(2)}, u32[]{:S(2)}) collective-permute-start(bf16[4,32,128]{2,1,0:T(8,128)(2,1)S(1)} %pad_maximum_fusion.1), channel_id=1, source_target_pairs={{0,4},{1,5},{2,6},{3,7},{4,0},{5,1},{6,2},{7,3},{8,12},{9,13},{10,... | collective-permute-start | bytes 98312 | tf_op jit(solution)/shard_map/ppermute | solution.py:130
  14.5 5.3 %collective-permute-start.3 = (bf16[8,32,128]{2,1,0:T(8,128)(2,1)S(1)}, bf16[8,32,128]{2,1,0:T(8,128)(2,1)S(1)}, u32[]{:S(2)}, u32[]{:S(2)}) collective-permute-start(bf16[8,32,128]{2,1,0:T(8,128)(2,1)S(1)} %pad_maximum_fusion), channel_id=1, source_target_pairs={{0,8},{1,9},{2,10},{3,11},{4,12},{5,13},{6,14},{7,15},{8,0},{9,1},... | collective-permute-start | bytes 196616 | tf_op jit(solution)/shard_map/ppermute | solution.py:130
  23.1 13.3 %all-to-all-start = ((f32[16,1,64]{2,1,0:T(1,128)}), f32[16,1,64]{2,1,0:T(1,128)S(1)}, u32[]{:S(2)}, u32[]{:S(2)}) async-start(f32[16,1,64]{2,1,0:T(1,128)} %bitcast.4), calls=%async_computation | async-start | bytes 16384 | tf_op jit(solution)/shard_map/all_to_all | solution.py:135
  36.4 0.6 %copy-start.3 = (f32[16,1,64]{2,1,0:T(1,128)}, f32[16,1,64]{2,1,0:T(1,128)S(1)}, u32[]{:S(2)}) copy-start(f32[16,1,64]{2,1,0:T(1,128)S(1)} %all-to-all-done) | copy-start | bytes 12292

commit v2 on v1

v2 whole, which is shorter than its diff:
```python
import functools

import jax
import jax.numpy as jnp
from jax import lax
from jax.experimental import pallas as pl
from jax.experimental.pallas import tpu as pltpu
from jax.sharding import PartitionSpec as P

PREFIX = 64
EPS = 1e-06
CHUNKS = 8
VMEM = pl.BlockSpec(memory_space=pltpu.VMEM)
ANY = pl.BlockSpec(memory_space=pl.ANY)
HBM = pl.BlockSpec(memory_space=pltpu.HBM)


def params(mib=16):
    return pltpu.CompilerParams(vmem_limit_bytes=mib << 20)


def unit_prefix(rows):
    head = rows[:, :PREFIX]
    total = jnp.sum(head * head, axis=-1, keepdims=True)
    return (head * lax.rsqrt(total + EPS)).astype(jnp.bfloat16)


def live_kernel(lens_hbm, passages_hbm, full_ref, lens_ref, passages_ref, sems):
    count, width, dim = passages_ref.shape
    size = count // CHUNKS
    lens_copy = pltpu.make_async_copy(lens_hbm, lens_ref, sems.at[CHUNKS])
    lens_copy.start()
    copies = []
    for c in range(CHUNKS):
        part = pl.ds(c * size, size)
        copies.append(pltpu.make_async_copy(passages_hbm.at[part], passages_ref.at[part], sems.at[c]))
        copies[-1].start()
    lens_copy.wait()
    row = lax.broadcasted_iota(jnp.int32, (width, dim), 0)
    for p in range(count):
        if p % size == 0:
            copies[p // size].wait()
        tokens = passages_ref[p].astype(jnp.float32)
        tokens = jnp.where(row < lens_ref[p], tokens, tokens[0:1])
        full_ref[pl.ds(p * width, width), :] = tokens.astype(jnp.bfloat16)


def live_tokens(lengths, passages):
    count, width, dim = passages.shape
    return pl.pallas_call(
        live_kernel,
        out_shape=jax.ShapeDtypeStruct((count * width, dim), jnp.bfloat16),
        in_specs=[HBM, HBM],
        out_specs=VMEM,
        scratch_shapes=[
            pltpu.SMEM((count,), jnp.int32),
            pltpu.VMEM((count, width, dim), jnp.bfloat16),
            pltpu.SemaphoreType.DMA((CHUNKS + 1,)),
        ],
        compiler_params=params(50),
        cost_estimate=pl.CostEstimate(flops=count * width * dim * 8, bytes_accessed=6 << 20, transcendentals=0),
    )(lengths, passages)


def prefix_kernel(full_ref, prefix_ref):
    width = 128
    for at in range(0, full_ref.shape[0], width):
        prefix_ref[at : at + width, :] = unit_prefix(full_ref[at : at + width, :].astype(jnp.float32))


def prefixes(full):
    return pl.pallas_call(
        prefix_kernel,
        out_shape=jax.ShapeDtypeStruct((full.shape[0], PREFIX), jnp.bfloat16),
        in_specs=[VMEM],
        out_specs=VMEM,
        compiler_params=params(),
        cost_estimate=pl.CostEstimate(flops=full.size * 8, bytes_accessed=4 << 20, transcendentals=0),
    )(full)


def maxima(tokens_ref, queries, best_ref, count, width):
    rows = queries.shape[0]
    step = min(256, rows)
    for at in range(0, rows, step):
        block = queries[at : at + step, :]
        for p in range(0, count, 2):
            scores = lax.dot_general(
                tokens_ref[p * width : (p + 2) * width, :],
                block,
                (((1,), (1,)), ((), ())),
                preferred_element_type=jnp.float32,
            )
            best_ref[p : p + 2, at : at + step] = jnp.max(scores.reshape(2, width, step), axis=1)


def select(chosen, values, contract):
    total = None
    for _ in range(3):
        term = values.astype(jnp.bfloat16)
        values = values - term.astype(jnp.float32)
        part = lax.dot_general(chosen, term, (contract, ((), ())), preferred_element_type=jnp.float32)
        total = part if total is None else total + part
    return total


def average(best, first, places, rows, me):
    qtok = best.shape[1] // places
    shape = (rows, best.shape[1])
    place = lax.broadcasted_iota(jnp.int32, shape, 1) // qtok + first
    row = lax.broadcasted_iota(jnp.int32, shape, 0)
    wanted = row + first if me is None else row ^ me
    chosen = jnp.where(place == wanted, 1.0 / qtok, 0.0).astype(jnp.bfloat16)
    return select(chosen, best[...], ((1,), (1,)))


def exact_kernel(tokens_ref, queries_ref, out_ref, best_ref):
    count, width = best_ref.shape[0], tokens_ref.shape[0] // best_ref.shape[0]
    places = out_ref.shape[0]
    maxima(tokens_ref, queries_ref[...], best_ref, count, width)
    out_ref[...] = average(best_ref, 0, places, places, None)


def coarse_kernel(first, places, after_ref, tokens_ref, queries_ref, *rest):
    out_ref, best_ref = rest[-2:]
    count, width = best_ref.shape[0], tokens_ref.shape[0] // best_ref.shape[0]
    maxima(tokens_ref, unit_prefix(queries_ref[...].astype(jnp.float32)), best_ref, count, width)
    result = average(best_ref, first, places, out_ref.shape[0], lax.axis_index("slab"))
    out_ref[...] = result if len(rest) == 2 else rest[0][...] + result


def score(kernel, rows, count, tokens, queries, after=(), partial=()):
    places, qtok, dim = queries.shape
    queries = queries.reshape(places * qtok, dim)
    return pl.pallas_call(
        kernel,
        out_shape=jax.ShapeDtypeStruct((rows, count), jnp.float32),
        in_specs=[ANY] * len(after) + [VMEM] * (2 + len(partial)),
        out_specs=VMEM,
        scratch_shapes=[pltpu.VMEM((count, places * qtok), jnp.float32)],
        compiler_params=params(),
        cost_estimate=pl.CostEstimate(
            flops=4 * tokens.shape[0] * places * qtok * 128, bytes_accessed=4 << 20, transcendentals=0
        ),
    )(*after, tokens, queries, *partial)


def pick_kernel(count, order, ids_ref, returned_ref, out_ref):
    ids = ids_ref[...]
    short = ids.shape[1]
    source = (ids // count) ^ lax.axis_index("slab")
    block, scale = jnp.zeros_like(ids), 1
    for low, size in reversed(order):
        block = block + ((source // low) % size) * scale
        scale *= size
    place = block * count + ids % count
    lanes = 128
    rows = returned_ref.shape[1] // lanes
    table = jnp.concatenate([returned_ref[:, r * lanes : (r + 1) * lanes] for r in range(rows)], axis=0)
    hot = lax.broadcasted_iota(jnp.int32, (lanes, short), 0) == place % lanes
    hot = jnp.where(hot, 1.0, 0.0).astype(jnp.bfloat16)
    column = None
    rest = table
    for _ in range(3):
        term = rest.astype(jnp.bfloat16)
        rest = rest - term.astype(jnp.float32)
        part = lax.dot_general(term, hot, (((1,), (0,)), ((), ())), preferred_element_type=jnp.float32)
        column = part if column is None else column + part
    mine = lax.broadcasted_iota(jnp.int32, (rows, short), 0) == place // lanes
    out_ref[...] = jnp.sum(jnp.where(mine, column, 0.0), axis=0, keepdims=True)


def exchange(array, offset, owners):
    return lax.ppermute(array, "slab", [(i, i ^ offset) for i in range(owners)])


def join(*parts):
    return jnp.concatenate(parts, axis=0)


def stages(owners):
    found, low = [], 1
    while low < owners:
        size = min(4, owners // low)
        found.append((low, size))
        low *= size
    return found


def per_device(queries, passages, lengths, shortlist):
    owners = lax.axis_size("slab")
    count = passages.shape[0]
    order = stages(owners)
    half = owners // 2
    held = queries
    full = near = far = kept = None
    for low, size in order:
        came = [exchange(held, low * k, owners) for k in range(1, size)]
        if low == 1:
            full = live_tokens(lengths, passages)
            came[-2], came[-1], full = lax.optimization_barrier((came[-2], came[-1], full))
        parts = [held] + came
        if low * size == owners:
            near = join(*parts[: size // 2])
            prefix = prefixes(full)
            kept = score(exact_kernel, half, count, full, near)
            parts[-1], kept, prefix = lax.optimization_barrier((parts[-1], kept, prefix))
            far = join(*parts[size // 2 :])
        else:
            held = join(*parts)
    sent = score(exact_kernel, half, count, full, far)
    coarse = None
    rows = join(kept, sent)
    for low, size in reversed(order):
        away = [exchange(rows[low * k : low * (k + 1)], low * k, owners) for k in reversed(range(1, size))]
        rows = jnp.concatenate([rows[:low]] + away[::-1], axis=1)
        if coarse is None:
            coarse = score(functools.partial(coarse_kernel, 0, half), owners, count, prefix, near, after=(sent,))
            coarse = score(
                functools.partial(coarse_kernel, half, half), owners, count, prefix, far, after=(sent,), partial=(coarse,)
            )
    picked = pl.pallas_call(
        functools.partial(pick_kernel, count, order),
        out_shape=jax.ShapeDtypeStruct(shortlist.shape, jnp.float32),
        in_specs=[VMEM, VMEM],
        out_specs=VMEM,
        compiler_params=params(),
    )(shortlist, rows)
    return (coarse.T, picked)


def solution(mesh):
    return jax.shard_map(
        per_device,
        mesh=mesh,
        in_specs=(
            P(("groups", "slab"), None, None),
            P(("groups", "slab"), None, None),
            P(("groups", "slab")),
            P(("groups", "slab"), None),
        ),
        out_specs=(P(("groups", "slab"), None), P(("groups", "slab"), None)),
        check_vma=False,
    )
```

time: 38.6 us -> 30.5 us (0.79)
  waiting for transfers between devices: 8.86 us -> 4.33 us
  local copies, waits for them, and re-layouts: 3.58 us -> 1.46 us
  starting transfers between devices: 15.1 us -> 13.8 us
    all_to_all x1 -> x0, starting transfers between devices: 6.86 us -> none  [per_device(): lax.all_to_all(found, 'slab', split_axis=0, concat_axis=0, tiled=True)]
    ppermute x4 -> x12, starting transfers between devices: 8.29 us -> 13.8 us  [exchange(): return lax.ppermute(array, 'slab', [(i, i ^ offset) for i in range(owners)])]
    all_to_all x1 -> x0, waiting for transfers between devices: 3.03 us -> none  [per_device(): lax.all_to_all(found, 'slab', split_axis=0, concat_axis=0, tiled=True)]
    unnamed x12 -> x8, local copies, waits for them, and re-layouts: 3.56 us -> 1.42 us
    ppermute x4 -> x12, waiting for transfers between devices: 5.83 us -> 4.33 us  [exchange(): return lax.ppermute(array, 'slab', [(i, i ^ offset) for i in range(owners)])]
    pallas_call x4 -> x7, Pallas kernels: 10.1 us -> 9.85 us  [the longest x4 6.32 us: score(): pl.pallas_call(kernel, out_shape=jax.ShapeDtypeStruct((rows, count), jnp....]
  transfers between devices with their start and end apart: 5 -> 12, of which waited for: 4 -> 4; matrix products, arithmetic and copies ran while one was open for 2% -> 2% of each run, Pallas kernels for 14% -> 26%
where the time goes in v2:
time: 30.5 us; the launch traced here: 30.3 us
  starting transfers between devices  13.8 us (45%)
  Pallas kernels  9.85 us (32%)
  waiting for transfers between devices  4.33 us (14%)
  local copies, waits for them, and re-layouts  1.46 us (5%)
  between operations  0.74 us (2%)
    ppermute x12, starting transfers between devices, exchange(): return lax.ppermute(array, 'slab', [(i, i ^ offset) for i in range(owners)])  13.8 us
    pallas_call x4, Pallas kernels, score(): pl.pallas_call(kernel, out_shape=jax.ShapeDtypeStruct((rows, count), jnp....  6.32 us
    ppermute x12, waiting for transfers between devices, exchange(): return lax.ppermute(array, 'slab', [(i, i ^ offset) for i in range(owners)])  4.33 us
    pallas_call x1, Pallas kernels, live_tokens(): pl.pallas_call(live_kernel, out_shape=jax.ShapeDtypeStruct((count * width...  1.64 us
    unnamed x8, local copies, waits for them, and re-layouts  1.42 us
    pallas_call x1, Pallas kernels, prefixes(): pl.pallas_call(prefix_kernel, out_shape=jax.ShapeDtypeStruct((full.shape[...  1.18 us
    pallas_call x1, Pallas kernels, per_device(): pl.pallas_call(functools.partial(pick_kernel, count, order), out_shape=ja...  0.7 us
  transfers between devices with their start and end apart: 12, of which 4 were waited for; matrix products, arithmetic and copies ran while one was open for 2% of the time, Pallas kernels for 26%

profile of v2, /device:TPU:0, one launch (start us, length us, event | category | flops | bytes accessed | tf_op | source)
XLA Modules:
  0.0 30.3 jit_solution(13379874148911659798)
XLA Ops:
  0.6 2.5 %collective-permute-start.1 = (bf16[1,32,128]{2,1,0:T(8,128)(2,1)}, bf16[1,32,128]{2,1,0:T(8,128)(2,1)S(1)}, u32[]{:S(2)}, u32[]{:S(2)}) collective-permute-start(bf16[1,32,128]{2,1,0:T(8,128)(2,1)} %param.4), channel_id=1, source_target_pairs={{0,3},{1,2},{2,1},{3,0},{4,7},{5,6},{6,5},{7,4},{8,11},{9,10},{10,... | collective-permute-start | bytes 24584 | tf_op jit(solution)/shard_map/ppermute | solution.py:174
  3.1 0.6 %collective-permute-start = (bf16[1,32,128]{2,1,0:T(8,128)(2,1)}, bf16[1,32,128]{2,1,0:T(8,128)(2,1)S(1)}, u32[]{:S(2)}, u32[]{:S(2)}) collective-permute-start(bf16[1,32,128]{2,1,0:T(8,128)(2,1)} %param.4), channel_id=1, source_target_pairs={{0,2},{1,3},{2,0},{3,1},{4,6},{5,7},{6,4},{7,5},{8,10},{9,11},{10,... | collective-permute-start | bytes 24584 | tf_op jit(solution)/shard_map/ppermute | solution.py:174
  3.8 0.7 %constant_dynamic-update-slice_fusion.8 = (bf16[8,32,128]{2,1,0:T(8,128)(2,1)S(1)}, bf16[4,32,128]{2,1,0:T(8,128)(2,1)S(1)}) fusion(bf16[1,32,128]{2,1,0:T(8,128)(2,1)} %param.4), kind=kLoop, calls=%fused_computation.9 | loop fusion | bytes 24576
  4.5 0.7 %copy-done = s32[64]{0:T(128)S(1)} copy-done((s32[64]{0:T(128)S(1)}, s32[64]{0:T(128)}, u32[]{:S(2)}) %copy-start) | copy-done | bytes 280
  5.2 1.6 %shard_map.59.tokens_ref.full_ref = bf16[8192,128]{1,0:T(8,128)(2,1)S(1)} custom-call(s32[64]{0:T(128)S(1)} %copy-done, bf16[64,128,128]{2,1,0:T(8,128)(2,1)} %passages_hbm.1), custom_call_target="tpu_custom_call" | custom-call | flops 8388608 | bytes 6291456 | tf_op jit(solution)/shard_map/pallas_call | solution.py:50
  6.8 0.1 collective-permute-done
  7.0 1.7 %collective-permute-start.5 = (bf16[4,32,128]{2,1,0:T(8,128)(2,1)S(1)}, bf16[4,32,128]{2,1,0:T(8,128)(2,1)S(1)}, u32[]{:S(2)}, u32[]{:S(2)}) collective-permute-start(bf16[4,32,128]{2,1,0:T(8,128)(2,1)S(1)} %get-tuple-element.15), channel_id=1, source_target_pairs={{0,4},{1,5},{2,6},{3,7},{4,0},{5,1},{6,2},{7,3},{8,12},{9,13},{10,... | collective-permute-start | bytes 98312 | tf_op jit(solution)/shard_map/ppermute | solution.py:174
  8.7 2.5 %collective-permute-start.4 = (bf16[4,32,128]{2,1,0:T(8,128)(2,1)S(1)}, bf16[4,32,128]{2,1,0:T(8,128)(2,1)S(1)}, u32[]{:S(2)}, u32[]{:S(2)}) collective-permute-start(bf16[4,32,128]{2,1,0:T(8,128)(2,1)S(1)} %get-tuple-element.15), channel_id=1, source_target_pairs={{0,12},{1,13},{2,14},{3,15},{4,8},{5,9},{6,10},{7,11},{8,4},{9,5},... | collective-permute-start | bytes 98312 | tf_op jit(solution)/shard_map/ppermute | solution.py:174
  11.2 0.1 collective-permute-start.3
  11.3 1.2 %shard_map.61.tokens_ref = bf16[8192,64]{1,0:T(8,128)(2,1)S(1)} custom-call(bf16[8192,128]{1,0:T(8,128)(2,1)S(1)} %shard_map.59.tokens_ref.full_ref), custom_call_target="tpu_custom_call" | custom-call | flops 8388608 | bytes 4194304 | tf_op jit(solution)/shard_map/pallas_call | solution.py:72
  12.5 1.4 %shard_map.60 = f32[8,64]{1,0:T(8,128)S(1)} custom-call(bf16[8192,128]{1,0:T(8,128)(2,1)S(1)} %shard_map.59.tokens_ref.full_ref, bf16[256,128]{1,0:T(8,128)(2,1)S(1)} %bitcast.5), custom_call_target="tpu_custom_call" | custom-call | flops 1073741824 | bytes 4194304 | tf_op jit(solution)/shard_map/pallas_call | solution.py:135
  13.9 0.5 %collective-permute-done.4 = bf16[4,32,128]{2,1,0:T(8,128)(2,1)S(1)} collective-permute-done((bf16[4,32,128]{2,1,0:T(8,128)(2,1)S(1)}, bf16[4,32,128]{2,1,0:T(8,128)(2,1)S(1)}, u32[]{:S(2)}, u32[]{:S(2)}) %collective-permute-start.4) | collective-permute-done | bytes 32800 | tf_op jit(solution)/shard_map/ppermute | solution.py:174
  14.4 1.9 %collective-permute-done.3 = bf16[4,32,128]{2,1,0:T(8,128)(2,1)S(1)} collective-permute-done((bf16[4,32,128]{2,1,0:T(8,128)(2,1)S(1)}, bf16[4,32,128]{2,1,0:T(8,128)(2,1)S(1)}, u32[]{:S(2)}, u32[]{:S(2)}) %collective-permute-start.3) | collective-permute-done | bytes 32800 | tf_op jit(solution)/shard_map/ppermute | solution.py:174
  16.4 1.4 %shard_map.62.after_ref = f32[8,64]{1,0:T(8,128)S(1)} custom-call(bf16[8192,128]{1,0:T(8,128)(2,1)S(1)} %shard_map.59.tokens_ref.full_ref, bf16[256,128]{1,0:T(8,128)(2,1)S(1)} %bitcast.3), custom_call_target="tpu_custom_call" | custom-call | flops 1073741824 | bytes 4194304 | tf_op jit(solution)/shard_map/pallas_call | solution.py:135
  17.8 0.5 %collective-permute-start.6 = (f32[4,64]{1,0:T(4,128)S(1)}, f32[4,64]{1,0:T(4,128)S(1)}, u32[]{:S(2)}, u32[]{:S(2)}) collective-permute-start(f32[4,64]{1,0:T(4,128)S(1)} %get-tuple-element.27), channel_id=1, source_target_pairs={{0,4},{1,5},{2,6},{3,7},{4,0},{5,1},{6,2},{7,3},{8,12},{9,13},{10,... | collective-permute-start | bytes 3080 | tf_op jit(solution)/shard_map/ppermute | solution.py:174
  18.3 1.8 %collective-permute-start.7 = (f32[4,64]{1,0:T(4,128)S(1)}, f32[4,64]{1,0:T(4,128)S(1)}, u32[]{:S(2)}, u32[]{:S(2)}) collective-permute-start(f32[4,64]{1,0:T(4,128)S(1)} %get-tuple-element.28), channel_id=1, source_target_pairs={{0,8},{1,9},{2,10},{3,11},{4,12},{5,13},{6,14},{7,15},{8,0},{9,1},... | collective-permute-start | bytes 3080 | tf_op jit(solution)/shard_map/ppermute | solution.py:174
  20.1 2.2 %collective-permute-start.8 = (f32[4,64]{1,0:T(4,128)S(1)}, f32[4,64]{1,0:T(4,128)S(1)}, u32[]{:S(2)}, u32[]{:S(2)}) collective-permute-start(f32[4,64]{1,0:T(4,128)S(1)} %get-tuple-element.29), channel_id=1, source_target_pairs={{0,12},{1,13},{2,14},{3,15},{4,8},{5,9},{6,10},{7,11},{8,4},{9,5},... | collective-permute-start | bytes 3080 | tf_op jit(solution)/shard_map/ppermute | solution.py:174
  22.2 1.5 %shard_map.63.rest_0_ = f32[16,64]{1,0:T(8,128)S(1)} custom-call(f32[8,64]{1,0:T(8,128)S(1)} %shard_map.62.after_ref, bf16[8192,64]{1,0:T(8,128)(2,1)S(1)} %shard_map.61.tokens_ref, bf16[256,128]{1,0:T(8,128)(2,1)S(1)} %bitcast.6), custom_call_target="tpu_custom_call" | custom-call | flops 1073741824 | bytes 4194304 | tf_op jit(solution)/shard_map/pallas_call | solution.py:135
  23.7 1.7 %collective-permute-done.8 = f32[4,64]{1,0:T(4,128)S(1)} collective-permute-done((f32[4,64]{1,0:T(4,128)S(1)}, f32[4,64]{1,0:T(4,128)S(1)}, u32[]{:S(2)}, u32[]{:S(2)}) %collective-permute-start.8) | collective-permute-done | bytes 1056 | tf_op jit(solution)/shard_map/ppermute | solution.py:174
  25.4 0.1 pad_maximum_fusion.1
  25.6 1.5 %collective-permute-start.10 = (f32[1,256]{1,0:T(1,128)S(1)}, f32[1,256]{1,0:T(1,128)S(1)}, u32[]{:S(2)}, u32[]{:S(2)}) collective-permute-start(f32[1,256]{1,0:T(1,128)S(1)} %get-tuple-element.24), channel_id=1, source_target_pairs={{0,2},{1,3},{2,0},{3,1},{4,6},{5,7},{6,4},{7,5},{8,10},{9,11},{10,... | collective-permute-start | bytes 3080 | tf_op jit(solution)/shard_map/ppermute | solution.py:174
  27.0 0.4 %collective-permute-start.9 = (f32[1,256]{1,0:T(1,128)S(1)}, f32[1,256]{1,0:T(1,128)S(1)}, u32[]{:S(2)}, u32[]{:S(2)}) collective-permute-start(f32[1,256]{1,0:T(1,128)S(1)} %get-tuple-element.25), channel_id=1, source_target_pairs={{0,1},{1,0},{2,3},{3,2},{4,5},{5,4},{6,7},{7,6},{8,9},{9,8},{10,11... | collective-permute-start | bytes 3080 | tf_op jit(solution)/shard_map/ppermute | solution.py:174
  27.4 2.1 %shard_map.64 = f32[16,64]{1,0:T(8,128)} custom-call(f32[8,64]{1,0:T(8,128)S(1)} %shard_map.62.after_ref, bf16[8192,64]{1,0:T(8,128)(2,1)S(1)} %shard_map.61.tokens_ref, bf16[256,128]{1,0:T(8,128)(2,1)S(1)} %bitcast.4, f32[16,64]{1,0:T(8,128)S(1)} %shard_map.63.rest_0_), custom_call_target="tpu_custom_call" | custom-call | flops 1073741824 | bytes 4194304 | tf_op jit(solution)/shard_map/pallas_call | solution.py:135
  29.6 0.7 %shard_map.65 = f32[1,96]{1,0:T(1,128)} custom-call(s32[1,96]{1,0:T(1,128)S(1)} %copy-done.1, f32[1,1024]{1,0:T(1,128)S(1)} %pad_maximum_fusion.2.returned_ref), custom_call_target="tpu_custom_call" | custom-call | tf_op jit(solution)/shard_map/pallas_call | solution.py:222
  (22 shorter events, 0.2 us)
Async XLA Ops:
  0.6 6.2 %collective-permute-start.1 = (bf16[1,32,128]{2,1,0:T(8,128)(2,1)}, bf16[1,32,128]{2,1,0:T(8,128)(2,1)S(1)}, u32[]{:S(2)}, u32[]{:S(2)}) collective-permute-start(bf16[1,32,128]{2,1,0:T(8,128)(2,1)} %param.4), channel_id=1, source_target_pairs={{0,3},{1,2},{2,1},{3,0},{4,7},{5,6},{6,5},{7,4},{8,11},{9,10},{10,... | collective-permute-start | bytes 24584 | tf_op jit(solution)/shard_map/ppermute | solution.py:174
  3.1 3.9 %collective-permute-start = (bf16[1,32,128]{2,1,0:T(8,128)(2,1)}, bf16[1,32,128]{2,1,0:T(8,128)(2,1)S(1)}, u32[]{:S(2)}, u32[]{:S(2)}) collective-permute-start(bf16[1,32,128]{2,1,0:T(8,128)(2,1)} %param.4), channel_id=1, source_target_pairs={{0,2},{1,3},{2,0},{3,1},{4,6},{5,7},{6,4},{7,5},{8,10},{9,11},{10,... | collective-permute-start | bytes 24584 | tf_op jit(solution)/shard_map/ppermute | solution.py:174
  3.7 3.2 %collective-permute-start.2 = (bf16[1,32,128]{2,1,0:T(8,128)(2,1)}, bf16[1,32,128]{2,1,0:T(8,128)(2,1)S(1)}, u32[]{:S(2)}, u32[]{:S(2)}) collective-permute-start(bf16[1,32,128]{2,1,0:T(8,128)(2,1)} %param.4), channel_id=1, source_target_pairs={{0,1},{1,0},{2,3},{3,2},{4,5},{5,4},{6,7},{7,6},{8,9},{9,8},{10,11... | collective-permute-start | bytes 24584 | tf_op jit(solution)/shard_map/ppermute | solution.py:174
  4.5 0.7 %copy-start = (s32[64]{0:T(128)S(1)}, s32[64]{0:T(128)}, u32[]{:S(2)}) copy-start(s32[64]{0:T(128)} %lens_hbm.1) | copy-start | bytes 772
  7.0 5.5 %collective-permute-start.5 = (bf16[4,32,128]{2,1,0:T(8,128)(2,1)S(1)}, bf16[4,32,128]{2,1,0:T(8,128)(2,1)S(1)}, u32[]{:S(2)}, u32[]{:S(2)}) collective-permute-start(bf16[4,32,128]{2,1,0:T(8,128)(2,1)S(1)} %get-tuple-element.15), channel_id=1, source_target_pairs={{0,4},{1,5},{2,6},{3,7},{4,0},{5,1},{6,2},{7,3},{8,12},{9,13},{10,... | collective-permute-start | bytes 98312 | tf_op jit(solution)/shard_map/ppermute | solution.py:174
  8.7 5.7 %collective-permute-start.4 = (bf16[4,32,128]{2,1,0:T(8,128)(2,1)S(1)}, bf16[4,32,128]{2,1,0:T(8,128)(2,1)S(1)}, u32[]{:S(2)}, u32[]{:S(2)}) collective-permute-start(bf16[4,32,128]{2,1,0:T(8,128)(2,1)S(1)} %get-tuple-element.15), channel_id=1, source_target_pairs={{0,12},{1,13},{2,14},{3,15},{4,8},{5,9},{6,10},{7,11},{8,4},{9,5},... | collective-permute-start | bytes 98312 | tf_op jit(solution)/shard_map/ppermute | solution.py:174
  11.2 5.2 %collective-permute-start.3 = (bf16[4,32,128]{2,1,0:T(8,128)(2,1)S(1)}, bf16[4,32,128]{2,1,0:T(8,128)(2,1)S(1)}, u32[]{:S(2)}, u32[]{:S(2)}) collective-permute-start(bf16[4,32,128]{2,1,0:T(8,128)(2,1)S(1)} %get-tuple-element.15), channel_id=1, source_target_pairs={{0,8},{1,9},{2,10},{3,11},{4,12},{5,13},{6,14},{7,15},{8,0},{9,1},... | collective-permute-start | bytes 98312 | tf_op jit(solution)/shard_map/ppermute | solution.py:174
  17.8 5.9 %collective-permute-start.6 = (f32[4,64]{1,0:T(4,128)S(1)}, f32[4,64]{1,0:T(4,128)S(1)}, u32[]{:S(2)}, u32[]{:S(2)}) collective-permute-start(f32[4,64]{1,0:T(4,128)S(1)} %get-tuple-element.27), channel_id=1, source_target_pairs={{0,4},{1,5},{2,6},{3,7},{4,0},{5,1},{6,2},{7,3},{8,12},{9,13},{10,... | collective-permute-start | bytes 3080 | tf_op jit(solution)/shard_map/ppermute | solution.py:174
  18.3 5.5 %collective-permute-start.7 = (f32[4,64]{1,0:T(4,128)S(1)}, f32[4,64]{1,0:T(4,128)S(1)}, u32[]{:S(2)}, u32[]{:S(2)}) collective-permute-start(f32[4,64]{1,0:T(4,128)S(1)} %get-tuple-element.28), channel_id=1, source_target_pairs={{0,8},{1,9},{2,10},{3,11},{4,12},{5,13},{6,14},{7,15},{8,0},{9,1},... | collective-permute-start | bytes 3080 | tf_op jit(solution)/shard_map/ppermute | solution.py:174
  20.1 5.4 %collective-permute-start.8 = (f32[4,64]{1,0:T(4,128)S(1)}, f32[4,64]{1,0:T(4,128)S(1)}, u32[]{:S(2)}, u32[]{:S(2)}) collective-permute-start(f32[4,64]{1,0:T(4,128)S(1)} %get-tuple-element.29), channel_id=1, source_target_pairs={{0,12},{1,13},{2,14},{3,15},{4,8},{5,9},{6,10},{7,11},{8,4},{9,5},... | collective-permute-start | bytes 3080 | tf_op jit(solution)/shard_map/ppermute | solution.py:174
  23.7 5.9 %copy-start.1 = (s32[1,96]{1,0:T(1,128)S(1)}, s32[1,96]{1,0:T(1,128)}, u32[]{:S(2)}) copy-start(s32[1,96]{1,0:T(1,128)} %ids_ref.1) | copy-start | bytes 1156
  25.5 4.0 %collective-permute-start.11 = (f32[1,256]{1,0:T(1,128)S(1)}, f32[1,256]{1,0:T(1,128)S(1)}, u32[]{:S(2)}, u32[]{:S(2)}) collective-permute-start(f32[1,256]{1,0:T(1,128)S(1)} %get-tuple-element.23), channel_id=1, source_target_pairs={{0,3},{1,2},{2,1},{3,0},{4,7},{5,6},{6,5},{7,4},{8,11},{9,10},{10,... | collective-permute-start | bytes 3080 | tf_op jit(solution)/shard_map/ppermute | solution.py:174
  25.6 4.0 %collective-permute-start.10 = (f32[1,256]{1,0:T(1,128)S(1)}, f32[1,256]{1,0:T(1,128)S(1)}, u32[]{:S(2)}, u32[]{:S(2)}) collective-permute-start(f32[1,256]{1,0:T(1,128)S(1)} %get-tuple-element.24), channel_id=1, source_target_pairs={{0,2},{1,3},{2,0},{3,1},{4,6},{5,7},{6,4},{7,5},{8,10},{9,11},{10,... | collective-permute-start | bytes 3080 | tf_op jit(solution)/shard_map/ppermute | solution.py:174
  27.0 2.5 %collective-permute-start.9 = (f32[1,256]{1,0:T(1,128)S(1)}, f32[1,256]{1,0:T(1,128)S(1)}, u32[]{:S(2)}, u32[]{:S(2)}) collective-permute-start(f32[1,256]{1,0:T(1,128)S(1)} %get-tuple-element.25), channel_id=1, source_target_pairs={{0,1},{1,0},{2,3},{3,2},{4,5},{5,4},{6,7},{7,6},{8,9},{9,8},{10,11... | collective-permute-start | bytes 3080 | tf_op jit(solution)/shard_map/ppermute | solution.py:174

commit v3 on v2

--- a/solution.py
+++ b/solution.py
@@ -104,28 +104,40 @@
     return total
 
 
-def average(best, first, places, rows, me):
+def average(best, first, places, rows, whose=None):
     qtok = best.shape[1] // places
     shape = (rows, best.shape[1])
     place = lax.broadcasted_iota(jnp.int32, shape, 1) // qtok + first
     row = lax.broadcasted_iota(jnp.int32, shape, 0)
-    wanted = row + first if me is None else row ^ me
-    chosen = jnp.where(place == wanted, 1.0 / qtok, 0.0).astype(jnp.bfloat16)
+    hit = place == row + first if whose is None else whose(place) == row
+    chosen = jnp.where(hit, 1.0 / qtok, 0.0).astype(jnp.bfloat16)
     return select(chosen, best[...], ((1,), (1,)))
+
+
+def regroup(place, order):
+    distance, below = jnp.zeros_like(place), 1
+    for low, size in order:
+        distance = distance + (place // below) % size * low
+        below *= size
+    return distance
 
 
 def exact_kernel(tokens_ref, queries_ref, out_ref, best_ref):
     count, width = best_ref.shape[0], tokens_ref.shape[0] // best_ref.shape[0]
     places = out_ref.shape[0]
     maxima(tokens_ref, queries_ref[...], best_ref, count, width)
-    out_ref[...] = average(best_ref, 0, places, places, None)
-
-
-def coarse_kernel(first, places, after_ref, tokens_ref, queries_ref, *rest):
+    out_ref[...] = average(best_ref, 0, places, places)
+
+
+def coarse_kernel(order, first, places, after_ref, tokens_ref, queries_ref, *rest):
     out_ref, best_ref = rest[-2:]
     count, width = best_ref.shape[0], tokens_ref.shape[0] // best_ref.shape[0]
     maxima(tokens_ref, unit_prefix(queries_ref[...].astype(jnp.float32)), best_ref, count, width)
-    result = average(best_ref, first, places, out_ref.shape[0], lax.axis_index("slab"))
+
+    def whose(place):
+        return regroup(place, order) ^ lax.axis_index("slab")
+
+    result = average(best_ref, first, places, out_ref.shape[0], whose)
     out_ref[...] = result if len(rest) == 2 else rest[0][...] + result
 
 
@@ -184,7 +196,7 @@
         size = min(4, owners // low)
         found.append((low, size))
         low *= size
-    return found
+    return found[::-1]
 
 
 def per_device(queries, passages, lengths, shortlist):
@@ -196,11 +208,11 @@
     full = near = far = kept = None
     for low, size in order:
         came = [exchange(held, low * k, owners) for k in range(1, size)]
-        if low == 1:
+        parts = [held] + came
+        if held is queries:
             full = live_tokens(lengths, passages)
-            came[-2], came[-1], full = lax.optimization_barrier((came[-2], came[-1], full))
-        parts = [held] + came
-        if low * size == owners:
+            parts[-2], parts[-1], full = lax.optimization_barrier((parts[-2], parts[-1], full))
+        if len(parts) * held.shape[0] == owners:
             near = join(*parts[: size // 2])
             prefix = prefixes(full)
             kept = score(exact_kernel, half, count, full, near)
@@ -212,13 +224,14 @@
     coarse = None
     rows = join(kept, sent)
     for low, size in reversed(order):
-        away = [exchange(rows[low * k : low * (k + 1)], low * k, owners) for k in reversed(range(1, size))]
-        rows = jnp.concatenate([rows[:low]] + away[::-1], axis=1)
+        group = rows.shape[0] // size
+        away = [exchange(rows[group * k : group * (k + 1)], low * k, owners) for k in reversed(range(1, size))]
+        rows = jnp.concatenate([rows[:group]] + away[::-1], axis=1)
         if coarse is None:
-            coarse = score(functools.partial(coarse_kernel, 0, half), owners, count, prefix, near, after=(sent,))
-            coarse = score(
-                functools.partial(coarse_kernel, half, half), owners, count, prefix, far, after=(sent,), partial=(coarse,)
-            )
+            near_kernel = functools.partial(coarse_kernel, order, 0, half)
+            far_kernel = functools.partial(coarse_kernel, order, half, half)
+            coarse = score(near_kernel, owners, count, prefix, near, after=(sent,))
+            coarse = score(far_kernel, owners, count, prefix, far, after=(sent,), partial=(coarse,))
     picked = pl.pallas_call(
         functools.partial(pick_kernel, count, order),
         out_shape=jax.ShapeDtypeStruct(shortlist.shape, jnp.float32),

time: 30.5 us -> 29.7 us (0.974)
  waiting for transfers between devices: 4.33 us -> 3.05 us
  starting transfers between devices: 13.8 us -> 14.3 us
    ppermute x12, waiting for transfers between devices: 4.33 us -> 3.05 us  [exchange(): return lax.ppermute(array, 'slab', [(i, i ^ offset) for i in range(owners)])]
    ppermute x12, starting transfers between devices: 13.8 us -> 14.3 us  [exchange(): return lax.ppermute(array, 'slab', [(i, i ^ offset) for i in range(owners)])]
  transfers between devices with their start and end apart: 12 -> 12, of which waited for: 4 -> 5; matrix products, arithmetic and copies ran while one was open for 2% -> 3% of each run, Pallas kernels for 26% -> 26%
where the time goes in v3:
time: 29.7 us; the launch traced here: 29.5 us
  starting transfers between devices  14.3 us (48%)
  Pallas kernels  9.86 us (33%)
  waiting for transfers between devices  3.05 us (10%)
  local copies, waits for them, and re-layouts  1.46 us (5%)
  between operations  0.74 us (2%)
    ppermute x12, starting transfers between devices, exchange(): return lax.ppermute(array, 'slab', [(i, i ^ offset) for i in range(owners)])  14.3 us
    pallas_call x4, Pallas kernels, score(): pl.pallas_call(kernel, out_shape=jax.ShapeDtypeStruct((rows, count), jnp....  6.33 us
    ppermute x12, waiting for transfers between devices, exchange(): return lax.ppermute(array, 'slab', [(i, i ^ offset) for i in range(owners)])  3.05 us
    pallas_call x1, Pallas kernels, live_tokens(): pl.pallas_call(live_kernel, out_shape=jax.ShapeDtypeStruct((count * width...  1.64 us
    unnamed x8, local copies, waits for them, and re-layouts  1.42 us
    pallas_call x1, Pallas kernels, prefixes(): pl.pallas_call(prefix_kernel, out_shape=jax.ShapeDtypeStruct((full.shape[...  1.18 us
    pallas_call x1, Pallas kernels, per_device(): pl.pallas_call(functools.partial(pick_kernel, count, order), out_shape=ja...  0.7 us
  transfers between devices with their start and end apart: 12, of which 5 were waited for; matrix products, arithmetic and copies ran while one was open for 3% of the time, Pallas kernels for 26%

profile of v3, /device:TPU:0, one launch (start us, length us, event | category | flops | bytes accessed | tf_op | source)
XLA Modules:
  0.0 29.5 jit_solution(266424168962264104)
XLA Ops:
  0.6 5.1 %collective-permute-start.1 = (bf16[1,32,128]{2,1,0:T(8,128)(2,1)}, bf16[1,32,128]{2,1,0:T(8,128)(2,1)S(1)}, u32[]{:S(2)}, u32[]{:S(2)}) collective-permute-start(bf16[1,32,128]{2,1,0:T(8,128)(2,1)} %param.4), channel_id=1, source_target_pairs={{0,12},{1,13},{2,14},{3,15},{4,8},{5,9},{6,10},{7,11},{8,4},{9,5},... | collective-permute-start | bytes 24584 | tf_op jit(solution)/shard_map/ppermute | solution.py:186
  5.7 0.6 %collective-permute-start.2 = (bf16[1,32,128]{2,1,0:T(8,128)(2,1)}, bf16[1,32,128]{2,1,0:T(8,128)(2,1)S(1)}, u32[]{:S(2)}, u32[]{:S(2)}) collective-permute-start(bf16[1,32,128]{2,1,0:T(8,128)(2,1)} %param.4), channel_id=1, source_target_pairs={{0,4},{1,5},{2,6},{3,7},{4,0},{5,1},{6,2},{7,3},{8,12},{9,13},{10,... | collective-permute-start | bytes 24584 | tf_op jit(solution)/shard_map/ppermute | solution.py:186
  6.4 0.7 %constant_dynamic-update-slice_fusion.8 = (bf16[8,32,128]{2,1,0:T(8,128)(2,1)S(1)}, bf16[4,32,128]{2,1,0:T(8,128)(2,1)S(1)}) fusion(bf16[1,32,128]{2,1,0:T(8,128)(2,1)} %param.4), kind=kLoop, calls=%fused_computation.9 | loop fusion | bytes 24576
  7.1 0.7 %copy-done = s32[64]{0:T(128)S(1)} copy-done((s32[64]{0:T(128)S(1)}, s32[64]{0:T(128)}, u32[]{:S(2)}) %copy-start) | copy-done | bytes 280
  7.8 1.6 %shard_map.59.tokens_ref.full_ref = bf16[8192,128]{1,0:T(8,128)(2,1)S(1)} custom-call(s32[64]{0:T(128)S(1)} %copy-done, bf16[64,128,128]{2,1,0:T(8,128)(2,1)} %passages_hbm.1), custom_call_target="tpu_custom_call" | custom-call | flops 8388608 | bytes 6291456 | tf_op jit(solution)/shard_map/pallas_call | solution.py:50
  9.4 1.1 %collective-permute-done = bf16[1,32,128]{2,1,0:T(8,128)(2,1)S(1)} collective-permute-done((bf16[1,32,128]{2,1,0:T(8,128)(2,1)}, bf16[1,32,128]{2,1,0:T(8,128)(2,1)S(1)}, u32[]{:S(2)}, u32[]{:S(2)}) %collective-permute-start) | collective-permute-done | bytes 8224 | tf_op jit(solution)/shard_map/ppermute | solution.py:186
  10.5 0.1 collective-permute-start.5
  10.6 1.6 %collective-permute-start.4 = (bf16[4,32,128]{2,1,0:T(8,128)(2,1)S(1)}, bf16[4,32,128]{2,1,0:T(8,128)(2,1)S(1)}, u32[]{:S(2)}, u32[]{:S(2)}) collective-permute-start(bf16[4,32,128]{2,1,0:T(8,128)(2,1)S(1)} %get-tuple-element.15), channel_id=1, source_target_pairs={{0,3},{1,2},{2,1},{3,0},{4,7},{5,6},{6,5},{7,4},{8,11},{9,10},{10,... | collective-permute-start | bytes 98312 | tf_op jit(solution)/shard_map/ppermute | solution.py:186
  12.3 0.5 %collective-permute-start.3 = (bf16[4,32,128]{2,1,0:T(8,128)(2,1)S(1)}, bf16[4,32,128]{2,1,0:T(8,128)(2,1)S(1)}, u32[]{:S(2)}, u32[]{:S(2)}) collective-permute-start(bf16[4,32,128]{2,1,0:T(8,128)(2,1)S(1)} %get-tuple-element.15), channel_id=1, source_target_pairs={{0,2},{1,3},{2,0},{3,1},{4,6},{5,7},{6,4},{7,5},{8,10},{9,11},{10,... | collective-permute-start | bytes 98312 | tf_op jit(solution)/shard_map/ppermute | solution.py:186
  12.8 1.2 %shard_map.61.tokens_ref = bf16[8192,64]{1,0:T(8,128)(2,1)S(1)} custom-call(bf16[8192,128]{1,0:T(8,128)(2,1)S(1)} %shard_map.59.tokens_ref.full_ref), custom_call_target="tpu_custom_call" | custom-call | flops 8388608 | bytes 4194304 | tf_op jit(solution)/shard_map/pallas_call | solution.py:72
  14.0 1.4 %shard_map.60 = f32[8,64]{1,0:T(8,128)S(1)} custom-call(bf16[8192,128]{1,0:T(8,128)(2,1)S(1)} %shard_map.59.tokens_ref.full_ref, bf16[256,128]{1,0:T(8,128)(2,1)S(1)} %bitcast.5), custom_call_target="tpu_custom_call" | custom-call | flops 1073741824 | bytes 4194304 | tf_op jit(solution)/shard_map/pallas_call | solution.py:147
  15.4 0.8 %collective-permute-done.3 = bf16[4,32,128]{2,1,0:T(8,128)(2,1)S(1)} collective-permute-done((bf16[4,32,128]{2,1,0:T(8,128)(2,1)S(1)}, bf16[4,32,128]{2,1,0:T(8,128)(2,1)S(1)}, u32[]{:S(2)}, u32[]{:S(2)}) %collective-permute-start.3) | collective-permute-done | bytes 32800 | tf_op jit(solution)/shard_map/ppermute | solution.py:186
  16.2 1.4 %shard_map.62.after_ref = f32[8,64]{1,0:T(8,128)S(1)} custom-call(bf16[8192,128]{1,0:T(8,128)(2,1)S(1)} %shard_map.59.tokens_ref.full_ref, bf16[256,128]{1,0:T(8,128)(2,1)S(1)} %bitcast.3), custom_call_target="tpu_custom_call" | custom-call | flops 1073741824 | bytes 4194304 | tf_op jit(solution)/shard_map/pallas_call | solution.py:147
  17.7 0.8 %collective-permute-start.7 = (f32[4,64]{1,0:T(4,128)S(1)}, f32[4,64]{1,0:T(4,128)S(1)}, u32[]{:S(2)}, u32[]{:S(2)}) collective-permute-start(f32[4,64]{1,0:T(4,128)S(1)} %get-tuple-element.28), channel_id=1, source_target_pairs={{0,2},{1,3},{2,0},{3,1},{4,6},{5,7},{6,4},{7,5},{8,10},{9,11},{10,... | collective-permute-start | bytes 3080 | tf_op jit(solution)/shard_map/ppermute | solution.py:186
  18.5 1.0 %collective-permute-start.8 = (f32[4,64]{1,0:T(4,128)S(1)}, f32[4,64]{1,0:T(4,128)S(1)}, u32[]{:S(2)}, u32[]{:S(2)}) collective-permute-start(f32[4,64]{1,0:T(4,128)S(1)} %get-tuple-element.29), channel_id=1, source_target_pairs={{0,3},{1,2},{2,1},{3,0},{4,7},{5,6},{6,5},{7,4},{8,11},{9,10},{10,... | collective-permute-start | bytes 3080 | tf_op jit(solution)/shard_map/ppermute | solution.py:186
  19.5 1.5 %shard_map.63.rest_0_ = f32[16,64]{1,0:T(8,128)S(1)} custom-call(f32[8,64]{1,0:T(8,128)S(1)} %shard_map.62.after_ref, bf16[8192,64]{1,0:T(8,128)(2,1)S(1)} %shard_map.61.tokens_ref, bf16[256,128]{1,0:T(8,128)(2,1)S(1)} %bitcast.6), custom_call_target="tpu_custom_call" | custom-call | flops 1073741824 | bytes 4194304 | tf_op jit(solution)/shard_map/pallas_call | solution.py:147
  21.0 0.3 collective-permute-done.7
  21.3 0.2 collective-permute-done.8
  21.5 0.1 pad_maximum_fusion.1
  21.6 2.7 %collective-permute-start.11 = (f32[1,256]{1,0:T(1,128)S(1)}, f32[1,256]{1,0:T(1,128)S(1)}, u32[]{:S(2)}, u32[]{:S(2)}) collective-permute-start(f32[1,256]{1,0:T(1,128)S(1)} %get-tuple-element.23), channel_id=1, source_target_pairs={{0,12},{1,13},{2,14},{3,15},{4,8},{5,9},{6,10},{7,11},{8,4},{9,5},... | collective-permute-start | bytes 3080 | tf_op jit(solution)/shard_map/ppermute | solution.py:186
  24.3 1.7 %collective-permute-start.9 = (f32[1,256]{1,0:T(1,128)S(1)}, f32[1,256]{1,0:T(1,128)S(1)}, u32[]{:S(2)}, u32[]{:S(2)}) collective-permute-start(f32[1,256]{1,0:T(1,128)S(1)} %get-tuple-element.25), channel_id=1, source_target_pairs={{0,4},{1,5},{2,6},{3,7},{4,0},{5,1},{6,2},{7,3},{8,12},{9,13},{10,... | collective-permute-start | bytes 3080 | tf_op jit(solution)/shard_map/ppermute | solution.py:186
  26.0 2.1 %shard_map.64 = f32[16,64]{1,0:T(8,128)} custom-call(f32[8,64]{1,0:T(8,128)S(1)} %shard_map.62.after_ref, bf16[8192,64]{1,0:T(8,128)(2,1)S(1)} %shard_map.61.tokens_ref, bf16[256,128]{1,0:T(8,128)(2,1)S(1)} %bitcast.4, f32[16,64]{1,0:T(8,128)S(1)} %shard_map.63.rest_0_), custom_call_target="tpu_custom_call" | custom-call | flops 1073741824 | bytes 4194304 | tf_op jit(solution)/shard_map/pallas_call | solution.py:147
  28.1 0.7 %collective-permute-done.10 = f32[1,256]{1,0:T(1,128)S(1)} collective-permute-done((f32[1,256]{1,0:T(1,128)S(1)}, f32[1,256]{1,0:T(1,128)S(1)}, u32[]{:S(2)}, u32[]{:S(2)}) %collective-permute-start.10) | collective-permute-done | bytes 1056 | tf_op jit(solution)/shard_map/ppermute | solution.py:186
  28.8 0.7 %shard_map.65 = f32[1,96]{1,0:T(1,128)} custom-call(s32[1,96]{1,0:T(1,128)S(1)} %copy-done.1, f32[1,1024]{1,0:T(1,128)S(1)} %pad_maximum_fusion.2.returned_ref), custom_call_target="tpu_custom_call" | custom-call | tf_op jit(solution)/shard_map/pallas_call | solution.py:235
  (22 shorter events, 0.2 us)
Async XLA Ops:
  0.6 8.8 %collective-permute-start.1 = (bf16[1,32,128]{2,1,0:T(8,128)(2,1)}, bf16[1,32,128]{2,1,0:T(8,128)(2,1)S(1)}, u32[]{:S(2)}, u32[]{:S(2)}) collective-permute-start(bf16[1,32,128]{2,1,0:T(8,128)(2,1)} %param.4), channel_id=1, source_target_pairs={{0,12},{1,13},{2,14},{3,15},{4,8},{5,9},{6,10},{7,11},{8,4},{9,5},... | collective-permute-start | bytes 24584 | tf_op jit(solution)/shard_map/ppermute | solution.py:186
  5.7 4.8 %collective-permute-start = (bf16[1,32,128]{2,1,0:T(8,128)(2,1)}, bf16[1,32,128]{2,1,0:T(8,128)(2,1)S(1)}, u32[]{:S(2)}, u32[]{:S(2)}) collective-permute-start(bf16[1,32,128]{2,1,0:T(8,128)(2,1)} %param.4), channel_id=1, source_target_pairs={{0,8},{1,9},{2,10},{3,11},{4,12},{5,13},{6,14},{7,15},{8,0},{9,1},... | collective-permute-start | bytes 24584 | tf_op jit(solution)/shard_map/ppermute | solution.py:186
  5.7 4.8 %collective-permute-start.2 = (bf16[1,32,128]{2,1,0:T(8,128)(2,1)}, bf16[1,32,128]{2,1,0:T(8,128)(2,1)S(1)}, u32[]{:S(2)}, u32[]{:S(2)}) collective-permute-start(bf16[1,32,128]{2,1,0:T(8,128)(2,1)} %param.4), channel_id=1, source_target_pairs={{0,4},{1,5},{2,6},{3,7},{4,0},{5,1},{6,2},{7,3},{8,12},{9,13},{10,... | collective-permute-start | bytes 24584 | tf_op jit(solution)/shard_map/ppermute | solution.py:186
  7.1 0.7 %copy-start = (s32[64]{0:T(128)S(1)}, s32[64]{0:T(128)}, u32[]{:S(2)}) copy-start(s32[64]{0:T(128)} %lens_hbm.1) | copy-start | bytes 772
  10.5 3.4 %collective-permute-start.5 = (bf16[4,32,128]{2,1,0:T(8,128)(2,1)S(1)}, bf16[4,32,128]{2,1,0:T(8,128)(2,1)S(1)}, u32[]{:S(2)}, u32[]{:S(2)}) collective-permute-start(bf16[4,32,128]{2,1,0:T(8,128)(2,1)S(1)} %get-tuple-element.15), channel_id=1, source_target_pairs={{0,1},{1,0},{2,3},{3,2},{4,5},{5,4},{6,7},{7,6},{8,9},{9,8},{10,11... | collective-permute-start | bytes 98312 | tf_op jit(solution)/shard_map/ppermute | solution.py:186
  10.6 4.7 %collective-permute-start.4 = (bf16[4,32,128]{2,1,0:T(8,128)(2,1)S(1)}, bf16[4,32,128]{2,1,0:T(8,128)(2,1)S(1)}, u32[]{:S(2)}, u32[]{:S(2)}) collective-permute-start(bf16[4,32,128]{2,1,0:T(8,128)(2,1)S(1)} %get-tuple-element.15), channel_id=1, source_target_pairs={{0,3},{1,2},{2,1},{3,0},{4,7},{5,6},{6,5},{7,4},{8,11},{9,10},{10,... | collective-permute-start | bytes 98312 | tf_op jit(solution)/shard_map/ppermute | solution.py:186
  12.3 3.9 %collective-permute-start.3 = (bf16[4,32,128]{2,1,0:T(8,128)(2,1)S(1)}, bf16[4,32,128]{2,1,0:T(8,128)(2,1)S(1)}, u32[]{:S(2)}, u32[]{:S(2)}) collective-permute-start(bf16[4,32,128]{2,1,0:T(8,128)(2,1)S(1)} %get-tuple-element.15), channel_id=1, source_target_pairs={{0,2},{1,3},{2,0},{3,1},{4,6},{5,7},{6,4},{7,5},{8,10},{9,11},{10,... | collective-permute-start | bytes 98312 | tf_op jit(solution)/shard_map/ppermute | solution.py:186
  17.6 3.4 %collective-permute-start.6 = (f32[4,64]{1,0:T(4,128)S(1)}, f32[4,64]{1,0:T(4,128)S(1)}, u32[]{:S(2)}, u32[]{:S(2)}) collective-permute-start(f32[4,64]{1,0:T(4,128)S(1)} %get-tuple-element.27), channel_id=1, source_target_pairs={{0,1},{1,0},{2,3},{3,2},{4,5},{5,4},{6,7},{7,6},{8,9},{9,8},{10,11... | collective-permute-start | bytes 3080 | tf_op jit(solution)/shard_map/ppermute | solution.py:186
  17.7 3.7 %collective-permute-start.7 = (f32[4,64]{1,0:T(4,128)S(1)}, f32[4,64]{1,0:T(4,128)S(1)}, u32[]{:S(2)}, u32[]{:S(2)}) collective-permute-start(f32[4,64]{1,0:T(4,128)S(1)} %get-tuple-element.28), channel_id=1, source_target_pairs={{0,2},{1,3},{2,0},{3,1},{4,6},{5,7},{6,4},{7,5},{8,10},{9,11},{10,... | collective-permute-start | bytes 3080 | tf_op jit(solution)/shard_map/ppermute | solution.py:186
  18.5 3.0 %collective-permute-start.8 = (f32[4,64]{1,0:T(4,128)S(1)}, f32[4,64]{1,0:T(4,128)S(1)}, u32[]{:S(2)}, u32[]{:S(2)}) collective-permute-start(f32[4,64]{1,0:T(4,128)S(1)} %get-tuple-element.29), channel_id=1, source_target_pairs={{0,3},{1,2},{2,1},{3,0},{4,7},{5,6},{6,5},{7,4},{8,11},{9,10},{10,... | collective-permute-start | bytes 3080 | tf_op jit(solution)/shard_map/ppermute | solution.py:186
  21.0 7.8 %copy-start.1 = (s32[1,96]{1,0:T(1,128)S(1)}, s32[1,96]{1,0:T(1,128)}, u32[]{:S(2)}) copy-start(s32[1,96]{1,0:T(1,128)} %ids_ref.1) | copy-start | bytes 1156
  21.6 6.5 %collective-permute-start.11 = (f32[1,256]{1,0:T(1,128)S(1)}, f32[1,256]{1,0:T(1,128)S(1)}, u32[]{:S(2)}, u32[]{:S(2)}) collective-permute-start(f32[1,256]{1,0:T(1,128)S(1)} %get-tuple-element.23), channel_id=1, source_target_pairs={{0,12},{1,13},{2,14},{3,15},{4,8},{5,9},{6,10},{7,11},{8,4},{9,5},... | collective-permute-start | bytes 3080 | tf_op jit(solution)/shard_map/ppermute | solution.py:186
  24.3 4.5 %collective-permute-start.10 = (f32[1,256]{1,0:T(1,128)S(1)}, f32[1,256]{1,0:T(1,128)S(1)}, u32[]{:S(2)}, u32[]{:S(2)}) collective-permute-start(f32[1,256]{1,0:T(1,128)S(1)} %get-tuple-element.24), channel_id=1, source_target_pairs={{0,8},{1,9},{2,10},{3,11},{4,12},{5,13},{6,14},{7,15},{8,0},{9,1},... | collective-permute-start | bytes 3080 | tf_op jit(solution)/shard_map/ppermute | solution.py:186
  24.3 4.5 %collective-permute-start.9 = (f32[1,256]{1,0:T(1,128)S(1)}, f32[1,256]{1,0:T(1,128)S(1)}, u32[]{:S(2)}, u32[]{:S(2)}) collective-permute-start(f32[1,256]{1,0:T(1,128)S(1)} %get-tuple-element.25), channel_id=1, source_target_pairs={{0,4},{1,5},{2,6},{3,7},{4,0},{5,1},{6,2},{7,3},{8,12},{9,13},{10,... | collective-permute-start | bytes 3080 | tf_op jit(solution)/shard_map/ppermute | solution.py:186

commit v4 on v3

--- a/solution.py
+++ b/solution.py
@@ -62,28 +62,29 @@
     )(lengths, passages)
 
 
-def prefix_kernel(full_ref, prefix_ref):
+def prefix_kernel(*refs):
+    full_ref, prefix_ref = refs[-2:]
     width = 128
     for at in range(0, full_ref.shape[0], width):
         prefix_ref[at : at + width, :] = unit_prefix(full_ref[at : at + width, :].astype(jnp.float32))
 
 
-def prefixes(full):
+def prefixes(after, full):
     return pl.pallas_call(
         prefix_kernel,
         out_shape=jax.ShapeDtypeStruct((full.shape[0], PREFIX), jnp.bfloat16),
-        in_specs=[VMEM],
+        in_specs=[ANY] * len(after) + [VMEM],
         out_specs=VMEM,
         compiler_params=params(),
         cost_estimate=pl.CostEstimate(flops=full.size * 8, bytes_accessed=4 << 20, transcendentals=0),
-    )(full)
+    )(*after, full)
 
 
 def maxima(tokens_ref, queries, best_ref, count, width):
     rows = queries.shape[0]
-    step = min(256, rows)
-    for at in range(0, rows, step):
-        block = queries[at : at + step, :]
+    for at in range(0, rows, 256):
+        block = queries[at : at + 256, :]
+        step = block.shape[0]
         for p in range(0, count, 2):
             scores = lax.dot_general(
                 tokens_ref[p * width : (p + 2) * width, :],
@@ -205,33 +206,30 @@
     order = stages(owners)
     half = owners // 2
     held = queries
-    full = near = far = kept = None
+    full = None
     for low, size in order:
         came = [exchange(held, low * k, owners) for k in range(1, size)]
         parts = [held] + came
         if held is queries:
             full = live_tokens(lengths, passages)
             parts[-2], parts[-1], full = lax.optimization_barrier((parts[-2], parts[-1], full))
-        if len(parts) * held.shape[0] == owners:
-            near = join(*parts[: size // 2])
-            prefix = prefixes(full)
-            kept = score(exact_kernel, half, count, full, near)
-            parts[-1], kept, prefix = lax.optimization_barrier((parts[-1], kept, prefix))
-            far = join(*parts[size // 2 :])
-        else:
+        if len(parts) * held.shape[0] < owners:
             held = join(*parts)
-    sent = score(exact_kernel, half, count, full, far)
+    scores = [score(exact_kernel, half, count, full, join(*parts[: size // 2]))]
+    for part in parts[size // 2 :]:
+        scores.append(score(exact_kernel, part.shape[0], count, full, part))
     coarse = None
-    rows = join(kept, sent)
+    rows = join(*scores)
     for low, size in reversed(order):
         group = rows.shape[0] // size
         away = [exchange(rows[group * k : group * (k + 1)], low * k, owners) for k in reversed(range(1, size))]
         rows = jnp.concatenate([rows[:group]] + away[::-1], axis=1)
         if coarse is None:
-            near_kernel = functools.partial(coarse_kernel, order, 0, half)
-            far_kernel = functools.partial(coarse_kernel, order, half, half)
-            coarse = score(near_kernel, owners, count, prefix, near, after=(sent,))
-            coarse = score(far_kernel, owners, count, prefix, far, after=(sent,), partial=(coarse,))
+            prefix = prefixes(scores, full)
+            near_kernel = functools.partial(coarse_kernel, order, 0, held.shape[0])
+            far_kernel = functools.partial(coarse_kernel, order, held.shape[0], owners - held.shape[0])
+            coarse = score(near_kernel, owners, count, prefix, held, after=(scores[-1],))
+            coarse = score(far_kernel, owners, count, prefix, join(*came), after=(scores[-1],), partial=(coarse,))
     picked = pl.pallas_call(
         functools.partial(pick_kernel, count, order),
         out_shape=jax.ShapeDtypeStruct(shortlist.shape, jnp.float32),

time: 29.7 us -> 29.2 us (0.983)
  waiting for transfers between devices: 3.05 us -> 2.21 us
  Pallas kernels: 9.86 us -> 10.2 us
    ppermute x12, waiting for transfers between devices: 3.05 us -> 2.21 us  [exchange(): return lax.ppermute(array, 'slab', [(i, i ^ offset) for i in range(owners)])]
    pallas_call x4 -> x5, Pallas kernels: 6.33 us -> 6.69 us  [score(): pl.pallas_call(kernel, out_shape=jax.ShapeDtypeStruct((rows, count), jnp....]
  transfers between devices with their start and end apart: 12 -> 12, of which waited for: 5 -> 2; matrix products, arithmetic and copies ran while one was open for 3% -> 3% of each run, Pallas kernels for 26% -> 30%
where the time goes in v4:
time: 29.2 us; the launch traced here: 29 us
  starting transfers between devices  14.3 us (49%)
  Pallas kernels  10.2 us (35%)
  waiting for transfers between devices  2.21 us (8%)
  local copies, waits for them, and re-layouts  1.44 us (5%)
  between operations  0.73 us (2%)
    ppermute x12, starting transfers between devices, exchange(): return lax.ppermute(array, 'slab', [(i, i ^ offset) for i in range(owners)])  14.3 us
    pallas_call x5, Pallas kernels, score(): pl.pallas_call(kernel, out_shape=jax.ShapeDtypeStruct((rows, count), jnp....  6.69 us
    ppermute x12, waiting for transfers between devices, exchange(): return lax.ppermute(array, 'slab', [(i, i ^ offset) for i in range(owners)])  2.21 us
    pallas_call x1, Pallas kernels, live_tokens(): pl.pallas_call(live_kernel, out_shape=jax.ShapeDtypeStruct((count * width...  1.64 us
    unnamed x8, local copies, waits for them, and re-layouts  1.42 us
    pallas_call x1, Pallas kernels, prefixes(): pl.pallas_call(prefix_kernel, out_shape=jax.ShapeDtypeStruct((full.shape[...  1.18 us
    pallas_call x1, Pallas kernels, per_device(): pl.pallas_call(functools.partial(pick_kernel, count, order), out_shape=ja...  0.7 us
  transfers between devices with their start and end apart: 12, of which 2 were waited for; matrix products, arithmetic and copies ran while one was open for 3% of the time, Pallas kernels for 30%

profile of v4, /device:TPU:0, one launch (start us, length us, event | category | flops | bytes accessed | tf_op | source)
XLA Modules:
  0.0 29.0 jit_solution(4268211140141301490)
XLA Ops:
  0.6 4.1 %collective-permute-start = (bf16[1,32,128]{2,1,0:T(8,128)(2,1)}, bf16[1,32,128]{2,1,0:T(8,128)(2,1)S(1)}, u32[]{:S(2)}, u32[]{:S(2)}) collective-permute-start(bf16[1,32,128]{2,1,0:T(8,128)(2,1)} %param.4), channel_id=1, source_target_pairs={{0,8},{1,9},{2,10},{3,11},{4,12},{5,13},{6,14},{7,15},{8,0},{9,1},... | collective-permute-start | bytes 24584 | tf_op jit(solution)/shard_map/ppermute | solution.py:187
  4.7 1.3 %collective-permute-start.1 = (bf16[1,32,128]{2,1,0:T(8,128)(2,1)}, bf16[1,32,128]{2,1,0:T(8,128)(2,1)S(1)}, u32[]{:S(2)}, u32[]{:S(2)}) collective-permute-start(bf16[1,32,128]{2,1,0:T(8,128)(2,1)} %param.4), channel_id=1, source_target_pairs={{0,12},{1,13},{2,14},{3,15},{4,8},{5,9},{6,10},{7,11},{8,4},{9,5},... | collective-permute-start | bytes 24584 | tf_op jit(solution)/shard_map/ppermute | solution.py:187
  6.1 0.2 collective-permute-start.2
  6.3 0.7 %constant_dynamic-update-slice_fusion.8 = (bf16[8,32,128]{2,1,0:T(8,128)(2,1)S(1)}, bf16[4,32,128]{2,1,0:T(8,128)(2,1)S(1)}) fusion(bf16[1,32,128]{2,1,0:T(8,128)(2,1)} %param.4), kind=kLoop, calls=%fused_computation.9 | loop fusion | bytes 24576
  7.0 0.7 %copy-done = s32[64]{0:T(128)S(1)} copy-done((s32[64]{0:T(128)S(1)}, s32[64]{0:T(128)}, u32[]{:S(2)}) %copy-start) | copy-done | bytes 280
  7.7 1.6 %shard_map.59.tokens_ref.refs_3_ = bf16[8192,128]{1,0:T(8,128)(2,1)S(1)} custom-call(s32[64]{0:T(128)S(1)} %copy-done, bf16[64,128,128]{2,1,0:T(8,128)(2,1)} %passages_hbm.1), custom_call_target="tpu_custom_call" | custom-call | flops 8388608 | bytes 6291456 | tf_op jit(solution)/shard_map/pallas_call | solution.py:50
  9.4 1.0 %collective-permute-done.1 = bf16[1,32,128]{2,1,0:T(8,128)(2,1)S(1)} collective-permute-done((bf16[1,32,128]{2,1,0:T(8,128)(2,1)}, bf16[1,32,128]{2,1,0:T(8,128)(2,1)S(1)}, u32[]{:S(2)}, u32[]{:S(2)}) %collective-permute-start.1) | collective-permute-done | bytes 8224 | tf_op jit(solution)/shard_map/ppermute | solution.py:187
  10.5 1.6 %collective-permute-start.3 = (bf16[4,32,128]{2,1,0:T(8,128)(2,1)S(1)}, bf16[4,32,128]{2,1,0:T(8,128)(2,1)S(1)}, u32[]{:S(2)}, u32[]{:S(2)}) collective-permute-start(bf16[4,32,128]{2,1,0:T(8,128)(2,1)S(1)} %get-tuple-element.9), channel_id=1, source_target_pairs={{0,3},{1,2},{2,1},{3,0},{4,7},{5,6},{6,5},{7,4},{8,11},{9,10},{10,... | collective-permute-start | bytes 98312 | tf_op jit(solution)/shard_map/ppermute | solution.py:187
  12.1 0.5 %collective-permute-start.5 = (bf16[4,32,128]{2,1,0:T(8,128)(2,1)S(1)}, bf16[4,32,128]{2,1,0:T(8,128)(2,1)S(1)}, u32[]{:S(2)}, u32[]{:S(2)}) collective-permute-start(bf16[4,32,128]{2,1,0:T(8,128)(2,1)S(1)} %get-tuple-element.9), channel_id=1, source_target_pairs={{0,2},{1,3},{2,0},{3,1},{4,6},{5,7},{6,4},{7,5},{8,10},{9,11},{10,... | collective-permute-start | bytes 98312 | tf_op jit(solution)/shard_map/ppermute | solution.py:187
  12.7 1.4 %shard_map.61.refs_0_ = f32[8,64]{1,0:T(8,128)S(1)} custom-call(bf16[8192,128]{1,0:T(8,128)(2,1)S(1)} %shard_map.59.tokens_ref.refs_3_, bf16[256,128]{1,0:T(8,128)(2,1)S(1)} %bitcast.10), custom_call_target="tpu_custom_call" | custom-call | flops 1073741824 | bytes 4194304 | tf_op jit(solution)/shard_map/pallas_call | solution.py:148
  14.1 0.9 %shard_map.60.refs_2_.after_ref = f32[4,64]{1,0:T(4,128)S(1)} custom-call(bf16[8192,128]{1,0:T(8,128)(2,1)S(1)} %shard_map.59.tokens_ref.refs_3_, bf16[128,128]{1,0:T(8,128)(2,1)S(1)} %bitcast.6), custom_call_target="tpu_custom_call" | custom-call | flops 536870912 | bytes 4194304 | tf_op jit(solution)/shard_map/pallas_call | solution.py:148
  14.9 1.1 %collective-permute-done.5 = bf16[4,32,128]{2,1,0:T(8,128)(2,1)S(1)} collective-permute-done((bf16[4,32,128]{2,1,0:T(8,128)(2,1)S(1)}, bf16[4,32,128]{2,1,0:T(8,128)(2,1)S(1)}, u32[]{:S(2)}, u32[]{:S(2)}) %collective-permute-start.5) | collective-permute-done | bytes 32800 | tf_op jit(solution)/shard_map/ppermute | solution.py:187
  16.1 0.8 %shard_map.62.refs_1_ = f32[4,64]{1,0:T(4,128)S(1)} custom-call(bf16[8192,128]{1,0:T(8,128)(2,1)S(1)} %shard_map.59.tokens_ref.refs_3_, bf16[128,128]{1,0:T(8,128)(2,1)S(1)} %bitcast.7), custom_call_target="tpu_custom_call" | custom-call | flops 536870912 | bytes 4194304 | tf_op jit(solution)/shard_map/pallas_call | solution.py:148
  16.9 0.4 %collective-permute-start.8 = (f32[4,64]{1,0:T(4,128)S(1)}, f32[4,64]{1,0:T(4,128)S(1)}, u32[]{:S(2)}, u32[]{:S(2)}) collective-permute-start(f32[4,64]{1,0:T(4,128)S(1)} %shard_map.60.refs_2_.after_ref), channel_id=1, source_target_pairs={{0,3},{1,2},{2,1},{3,0},{4,7},{5,6},{6,5},{7,4},{8,11},{9,10},{10,... | collective-permute-start | bytes 3080 | tf_op jit(solution)/shard_map/ppermute | solution.py:187
  17.3 0.4 %collective-permute-start.7 = (f32[4,64]{1,0:T(4,128)S(1)}, f32[4,64]{1,0:T(4,128)S(1)}, u32[]{:S(2)}, u32[]{:S(2)}) collective-permute-start(f32[4,64]{1,0:T(4,128)S(1)} %shard_map.62.refs_1_), channel_id=1, source_target_pairs={{0,2},{1,3},{2,0},{3,1},{4,6},{5,7},{6,4},{7,5},{8,10},{9,11},{10,... | collective-permute-start | bytes 3080 | tf_op jit(solution)/shard_map/ppermute | solution.py:187
  17.7 1.2 %shard_map.63.tokens_ref = bf16[8192,64]{1,0:T(8,128)(2,1)S(1)} custom-call(f32[8,64]{1,0:T(8,128)S(1)} %shard_map.61.refs_0_, f32[4,64]{1,0:T(4,128)S(1)} %shard_map.62.refs_1_, f32[4,64]{1,0:T(4,128)S(1)} %shard_map.60.refs_2_.after_ref, bf16[8192,128]{1,0:T(8,128)(2,1)S(1)} %shard_map.59.tokens_ref.refs_3_), custom_call_target="tpu_custom_call" | custom-call | flops 8388608 | bytes 4194304 | tf_op jit(solution)/shard_map/pallas_call | solution.py:73
  18.9 1.1 %collective-permute-start.6 = (f32[4,64]{1,0:T(4,128)S(1)}, f32[4,64]{1,0:T(4,128)S(1)}, u32[]{:S(2)}, u32[]{:S(2)}) collective-permute-start(f32[4,64]{1,0:T(4,128)S(1)} %get-tuple-element.21), channel_id=1, source_target_pairs={{0,1},{1,0},{2,3},{3,2},{4,5},{5,4},{6,7},{7,6},{8,9},{9,8},{10,11... | collective-permute-start | bytes 3080 | tf_op jit(solution)/shard_map/ppermute | solution.py:187
  20.1 0.9 %shard_map.64.rest_0_ = f32[16,64]{1,0:T(8,128)S(1)} custom-call(f32[4,64]{1,0:T(4,128)S(1)} %shard_map.60.refs_2_.after_ref, bf16[8192,64]{1,0:T(8,128)(2,1)S(1)} %shard_map.63.tokens_ref, bf16[128,128]{1,0:T(8,128)(2,1)S(1)} %bitcast.9), custom_call_target="tpu_custom_call" | custom-call | flops 536870912 | bytes 4194304 | tf_op jit(solution)/shard_map/pallas_call | solution.py:148
  21.0 0.1 pad_maximum_fusion.1
  21.1 2.0 %collective-permute-start.11 = (f32[1,256]{1,0:T(1,128)S(1)}, f32[1,256]{1,0:T(1,128)S(1)}, u32[]{:S(2)}, u32[]{:S(2)}) collective-permute-start(f32[1,256]{1,0:T(1,128)S(1)} %get-tuple-element.17), channel_id=1, source_target_pairs={{0,12},{1,13},{2,14},{3,15},{4,8},{5,9},{6,10},{7,11},{8,4},{9,5},... | collective-permute-start | bytes 3080 | tf_op jit(solution)/shard_map/ppermute | solution.py:187
  23.2 0.3 collective-permute-start.10
  23.4 2.1 %collective-permute-start.9 = (f32[1,256]{1,0:T(1,128)S(1)}, f32[1,256]{1,0:T(1,128)S(1)}, u32[]{:S(2)}, u32[]{:S(2)}) collective-permute-start(f32[1,256]{1,0:T(1,128)S(1)} %get-tuple-element.19), channel_id=1, source_target_pairs={{0,4},{1,5},{2,6},{3,7},{4,0},{5,1},{6,2},{7,3},{8,12},{9,13},{10,... | collective-permute-start | bytes 3080 | tf_op jit(solution)/shard_map/ppermute | solution.py:187
  25.6 2.7 %shard_map.65 = f32[16,64]{1,0:T(8,128)} custom-call(f32[4,64]{1,0:T(4,128)S(1)} %shard_map.60.refs_2_.after_ref, bf16[8192,64]{1,0:T(8,128)(2,1)S(1)} %shard_map.63.tokens_ref, bf16[384,128]{1,0:T(8,128)(2,1)S(1)} %bitcast.8, f32[16,64]{1,0:T(8,128)S(1)} %shard_map.64.rest_0_), custom_call_target="tpu_custom_call" | custom-call | flops 1610612736 | bytes 4194304 | tf_op jit(solution)/shard_map/pallas_call | solution.py:148
  28.3 0.7 %shard_map.66 = f32[1,96]{1,0:T(1,128)} custom-call(s32[1,96]{1,0:T(1,128)S(1)} %copy-done.1, f32[1,1024]{1,0:T(1,128)S(1)} %pad_maximum_fusion.2.returned_ref), custom_call_target="tpu_custom_call" | custom-call | tf_op jit(solution)/shard_map/pallas_call | solution.py:233
  (22 shorter events, 0.2 us)
Async XLA Ops:
  0.6 8.7 %collective-permute-start = (bf16[1,32,128]{2,1,0:T(8,128)(2,1)}, bf16[1,32,128]{2,1,0:T(8,128)(2,1)S(1)}, u32[]{:S(2)}, u32[]{:S(2)}) collective-permute-start(bf16[1,32,128]{2,1,0:T(8,128)(2,1)} %param.4), channel_id=1, source_target_pairs={{0,8},{1,9},{2,10},{3,11},{4,12},{5,13},{6,14},{7,15},{8,0},{9,1},... | collective-permute-start | bytes 24584 | tf_op jit(solution)/shard_map/ppermute | solution.py:187
  4.7 5.7 %collective-permute-start.1 = (bf16[1,32,128]{2,1,0:T(8,128)(2,1)}, bf16[1,32,128]{2,1,0:T(8,128)(2,1)S(1)}, u32[]{:S(2)}, u32[]{:S(2)}) collective-permute-start(bf16[1,32,128]{2,1,0:T(8,128)(2,1)} %param.4), channel_id=1, source_target_pairs={{0,12},{1,13},{2,14},{3,15},{4,8},{5,9},{6,10},{7,11},{8,4},{9,5},... | collective-permute-start | bytes 24584 | tf_op jit(solution)/shard_map/ppermute | solution.py:187
  6.1 4.3 %collective-permute-start.2 = (bf16[1,32,128]{2,1,0:T(8,128)(2,1)}, bf16[1,32,128]{2,1,0:T(8,128)(2,1)S(1)}, u32[]{:S(2)}, u32[]{:S(2)}) collective-permute-start(bf16[1,32,128]{2,1,0:T(8,128)(2,1)} %param.4), channel_id=1, source_target_pairs={{0,4},{1,5},{2,6},{3,7},{4,0},{5,1},{6,2},{7,3},{8,12},{9,13},{10,... | collective-permute-start | bytes 24584 | tf_op jit(solution)/shard_map/ppermute | solution.py:187
  7.0 0.7 %copy-start = (s32[64]{0:T(128)S(1)}, s32[64]{0:T(128)}, u32[]{:S(2)}) copy-start(s32[64]{0:T(128)} %lens_hbm.1) | copy-start | bytes 772
  10.4 2.2 %collective-permute-start.4 = (bf16[4,32,128]{2,1,0:T(8,128)(2,1)S(1)}, bf16[4,32,128]{2,1,0:T(8,128)(2,1)S(1)}, u32[]{:S(2)}, u32[]{:S(2)}) collective-permute-start(bf16[4,32,128]{2,1,0:T(8,128)(2,1)S(1)} %get-tuple-element.9), channel_id=1, source_target_pairs={{0,1},{1,0},{2,3},{3,2},{4,5},{5,4},{6,7},{7,6},{8,9},{9,8},{10,11... | collective-permute-start | bytes 98312 | tf_op jit(solution)/shard_map/ppermute | solution.py:187
  10.5 3.5 %collective-permute-start.3 = (bf16[4,32,128]{2,1,0:T(8,128)(2,1)S(1)}, bf16[4,32,128]{2,1,0:T(8,128)(2,1)S(1)}, u32[]{:S(2)}, u32[]{:S(2)}) collective-permute-start(bf16[4,32,128]{2,1,0:T(8,128)(2,1)S(1)} %get-tuple-element.9), channel_id=1, source_target_pairs={{0,3},{1,2},{2,1},{3,0},{4,7},{5,6},{6,5},{7,4},{8,11},{9,10},{10,... | collective-permute-start | bytes 98312 | tf_op jit(solution)/shard_map/ppermute | solution.py:187
  12.1 3.9 %collective-permute-start.5 = (bf16[4,32,128]{2,1,0:T(8,128)(2,1)S(1)}, bf16[4,32,128]{2,1,0:T(8,128)(2,1)S(1)}, u32[]{:S(2)}, u32[]{:S(2)}) collective-permute-start(bf16[4,32,128]{2,1,0:T(8,128)(2,1)S(1)} %get-tuple-element.9), channel_id=1, source_target_pairs={{0,2},{1,3},{2,0},{3,1},{4,6},{5,7},{6,4},{7,5},{8,10},{9,11},{10,... | collective-permute-start | bytes 98312 | tf_op jit(solution)/shard_map/ppermute | solution.py:187
  16.9 4.1 %collective-permute-start.8 = (f32[4,64]{1,0:T(4,128)S(1)}, f32[4,64]{1,0:T(4,128)S(1)}, u32[]{:S(2)}, u32[]{:S(2)}) collective-permute-start(f32[4,64]{1,0:T(4,128)S(1)} %shard_map.60.refs_2_.after_ref), channel_id=1, source_target_pairs={{0,3},{1,2},{2,1},{3,0},{4,7},{5,6},{6,5},{7,4},{8,11},{9,10},{10,... | collective-permute-start | bytes 3080 | tf_op jit(solution)/shard_map/ppermute | solution.py:187
  17.3 3.7 %collective-permute-start.7 = (f32[4,64]{1,0:T(4,128)S(1)}, f32[4,64]{1,0:T(4,128)S(1)}, u32[]{:S(2)}, u32[]{:S(2)}) collective-permute-start(f32[4,64]{1,0:T(4,128)S(1)} %shard_map.62.refs_1_), channel_id=1, source_target_pairs={{0,2},{1,3},{2,0},{3,1},{4,6},{5,7},{6,4},{7,5},{8,10},{9,11},{10,... | collective-permute-start | bytes 3080 | tf_op jit(solution)/shard_map/ppermute | solution.py:187
  18.9 2.1 %collective-permute-start.6 = (f32[4,64]{1,0:T(4,128)S(1)}, f32[4,64]{1,0:T(4,128)S(1)}, u32[]{:S(2)}, u32[]{:S(2)}) collective-permute-start(f32[4,64]{1,0:T(4,128)S(1)} %get-tuple-element.21), channel_id=1, source_target_pairs={{0,1},{1,0},{2,3},{3,2},{4,5},{5,4},{6,7},{7,6},{8,9},{9,8},{10,11... | collective-permute-start | bytes 3080 | tf_op jit(solution)/shard_map/ppermute | solution.py:187
  21.1 7.1 %collective-permute-start.11 = (f32[1,256]{1,0:T(1,128)S(1)}, f32[1,256]{1,0:T(1,128)S(1)}, u32[]{:S(2)}, u32[]{:S(2)}) collective-permute-start(f32[1,256]{1,0:T(1,128)S(1)} %get-tuple-element.17), channel_id=1, source_target_pairs={{0,12},{1,13},{2,14},{3,15},{4,8},{5,9},{6,10},{7,11},{8,4},{9,5},... | collective-permute-start | bytes 3080 | tf_op jit(solution)/shard_map/ppermute | solution.py:187
  23.2 5.1 %collective-permute-start.10 = (f32[1,256]{1,0:T(1,128)S(1)}, f32[1,256]{1,0:T(1,128)S(1)}, u32[]{:S(2)}, u32[]{:S(2)}) collective-permute-start(f32[1,256]{1,0:T(1,128)S(1)} %get-tuple-element.18), channel_id=1, source_target_pairs={{0,8},{1,9},{2,10},{3,11},{4,12},{5,13},{6,14},{7,15},{8,0},{9,1},... | collective-permute-start | bytes 3080 | tf_op jit(solution)/shard_map/ppermute | solution.py:187
  23.4 4.8 %collective-permute-start.9 = (f32[1,256]{1,0:T(1,128)S(1)}, f32[1,256]{1,0:T(1,128)S(1)}, u32[]{:S(2)}, u32[]{:S(2)}) collective-permute-start(f32[1,256]{1,0:T(1,128)S(1)} %get-tuple-element.19), channel_id=1, source_target_pairs={{0,4},{1,5},{2,6},{3,7},{4,0},{5,1},{6,2},{7,3},{8,12},{9,13},{10,... | collective-permute-start | bytes 3080 | tf_op jit(solution)/shard_map/ppermute | solution.py:187
  25.6 2.7 %copy-start.1 = (s32[1,96]{1,0:T(1,128)S(1)}, s32[1,96]{1,0:T(1,128)}, u32[]{:S(2)}) copy-start(s32[1,96]{1,0:T(1,128)} %ids_ref.1) | copy-start | bytes 1156

commit v5 on v4

--- a/solution.py
+++ b/solution.py
@@ -158,7 +158,10 @@
     )(*after, tokens, queries, *partial)
 
 
-def pick_kernel(count, order, ids_ref, returned_ref, out_ref):
+def pick_kernel(count, order, coarse_ref, ids_ref, returned_ref, exact_out, coarse_out, picked_ref, sems):
+    coarse_copy = pltpu.make_async_copy(coarse_ref, coarse_out, sems.at[0])
+    exact_copy = pltpu.make_async_copy(picked_ref, exact_out, sems.at[1])
+    coarse_copy.start()
     ids = ids_ref[...]
     short = ids.shape[1]
     source = (ids // count) ^ lax.axis_index("slab")
@@ -180,7 +183,10 @@
         part = lax.dot_general(term, hot, (((1,), (0,)), ((), ())), preferred_element_type=jnp.float32)
         column = part if column is None else column + part
     mine = lax.broadcasted_iota(jnp.int32, (rows, short), 0) == place // lanes
-    out_ref[...] = jnp.sum(jnp.where(mine, column, 0.0), axis=0, keepdims=True)
+    picked_ref[...] = jnp.sum(jnp.where(mine, column, 0.0), axis=0, keepdims=True)
+    exact_copy.start()
+    coarse_copy.wait()
+    exact_copy.wait()
 
 
 def exchange(array, offset, owners):
@@ -230,14 +236,18 @@
             far_kernel = functools.partial(coarse_kernel, order, held.shape[0], owners - held.shape[0])
             coarse = score(near_kernel, owners, count, prefix, held, after=(scores[-1],))
             coarse = score(far_kernel, owners, count, prefix, join(*came), after=(scores[-1],), partial=(coarse,))
-    picked = pl.pallas_call(
+    exact, coarse = pl.pallas_call(
         functools.partial(pick_kernel, count, order),
-        out_shape=jax.ShapeDtypeStruct(shortlist.shape, jnp.float32),
-        in_specs=[VMEM, VMEM],
-        out_specs=VMEM,
+        out_shape=(
+            jax.ShapeDtypeStruct(shortlist.shape, jnp.float32),
+            jax.ShapeDtypeStruct(coarse.shape, jnp.float32),
+        ),
+        in_specs=[VMEM, VMEM, VMEM],
+        out_specs=(ANY, ANY),
+        scratch_shapes=[pltpu.VMEM(shortlist.shape, jnp.float32), pltpu.SemaphoreType.DMA((2,))],
         compiler_params=params(),
-    )(shortlist, rows)
-    return (coarse.T, picked)
+    )(coarse, shortlist, rows)
+    return (coarse.T, exact)
 
 
 def solution(mesh):

time: 29.2 us -> 28.6 us (0.979)
  Pallas kernels: 10.2 us -> 9.61 us
    pallas_call x5, Pallas kernels: 6.69 us -> 6.07 us  [score(): pl.pallas_call(kernel, out_shape=jax.ShapeDtypeStruct((rows, count), jnp....]
  transfers between devices with their start and end apart: 12 -> 12, of which waited for: 2 -> 2; matrix products, arithmetic and copies ran while one was open for 3% -> 3% of each run, Pallas kernels for 30% -> 28%
where the time goes in v5:
time: 28.6 us; the launch traced here: 28.4 us
  starting transfers between devices  14.3 us (50%)
  Pallas kernels  9.61 us (34%)
  waiting for transfers between devices  2.24 us (8%)
  local copies, waits for them, and re-layouts  1.44 us (5%)
  between operations  0.73 us (3%)
    ppermute x12, starting transfers between devices, exchange(): return lax.ppermute(array, 'slab', [(i, i ^ offset) for i in range(owners)])  14.3 us
    pallas_call x5, Pallas kernels, score(): pl.pallas_call(kernel, out_shape=jax.ShapeDtypeStruct((rows, count), jnp....  6.07 us
    ppermute x12, waiting for transfers between devices, exchange(): return lax.ppermute(array, 'slab', [(i, i ^ offset) for i in range(owners)])  2.24 us
    pallas_call x1, Pallas kernels, live_tokens(): pl.pallas_call(live_kernel, out_shape=jax.ShapeDtypeStruct((count * width...  1.64 us
    unnamed x8, local copies, waits for them, and re-layouts  1.42 us
    pallas_call x1, Pallas kernels, prefixes(): pl.pallas_call(prefix_kernel, out_shape=jax.ShapeDtypeStruct((full.shape[...  1.18 us
    pallas_call x1, Pallas kernels, per_device(): pl.pallas_call(functools.partial(pick_kernel, count, order), out_shape=(j...  0.72 us
  transfers between devices with their start and end apart: 12, of which 2 were waited for; matrix products, arithmetic and copies ran while one was open for 3% of the time, Pallas kernels for 28%

profile of v5, /device:TPU:0, one launch (start us, length us, event | category | flops | bytes accessed | tf_op | source)
XLA Modules:
  0.0 28.4 jit_solution(7836948402235761166)
XLA Ops:
  0.6 4.1 %collective-permute-start = (bf16[1,32,128]{2,1,0:T(8,128)(2,1)}, bf16[1,32,128]{2,1,0:T(8,128)(2,1)S(1)}, u32[]{:S(2)}, u32[]{:S(2)}) collective-permute-start(bf16[1,32,128]{2,1,0:T(8,128)(2,1)} %param.4), channel_id=1, source_target_pairs={{0,8},{1,9},{2,10},{3,11},{4,12},{5,13},{6,14},{7,15},{8,0},{9,1},... | collective-permute-start | bytes 24584 | tf_op jit(solution)/shard_map/ppermute | solution.py:193
  4.7 1.3 %collective-permute-start.1 = (bf16[1,32,128]{2,1,0:T(8,128)(2,1)}, bf16[1,32,128]{2,1,0:T(8,128)(2,1)S(1)}, u32[]{:S(2)}, u32[]{:S(2)}) collective-permute-start(bf16[1,32,128]{2,1,0:T(8,128)(2,1)} %param.4), channel_id=1, source_target_pairs={{0,12},{1,13},{2,14},{3,15},{4,8},{5,9},{6,10},{7,11},{8,4},{9,5},... | collective-permute-start | bytes 24584 | tf_op jit(solution)/shard_map/ppermute | solution.py:193
  6.1 0.2 collective-permute-start.2
  6.3 0.7 %constant_dynamic-update-slice_fusion.8 = (bf16[8,32,128]{2,1,0:T(8,128)(2,1)S(1)}, bf16[4,32,128]{2,1,0:T(8,128)(2,1)S(1)}) fusion(bf16[1,32,128]{2,1,0:T(8,128)(2,1)} %param.4), kind=kLoop, calls=%fused_computation.9 | loop fusion | bytes 24576
  7.0 0.7 %copy-done = s32[64]{0:T(128)S(1)} copy-done((s32[64]{0:T(128)S(1)}, s32[64]{0:T(128)}, u32[]{:S(2)}) %copy-start) | copy-done | bytes 280
  7.7 1.6 %shard_map.59.tokens_ref.refs_3_ = bf16[8192,128]{1,0:T(8,128)(2,1)S(1)} custom-call(s32[64]{0:T(128)S(1)} %copy-done, bf16[64,128,128]{2,1,0:T(8,128)(2,1)} %passages_hbm.1), custom_call_target="tpu_custom_call" | custom-call | flops 8388608 | bytes 6291456 | tf_op jit(solution)/shard_map/pallas_call | solution.py:50
  9.4 1.0 %collective-permute-done.1 = bf16[1,32,128]{2,1,0:T(8,128)(2,1)S(1)} collective-permute-done((bf16[1,32,128]{2,1,0:T(8,128)(2,1)}, bf16[1,32,128]{2,1,0:T(8,128)(2,1)S(1)}, u32[]{:S(2)}, u32[]{:S(2)}) %collective-permute-start.1) | collective-permute-done | bytes 8224 | tf_op jit(solution)/shard_map/ppermute | solution.py:193
  10.5 1.6 %collective-permute-start.3 = (bf16[4,32,128]{2,1,0:T(8,128)(2,1)S(1)}, bf16[4,32,128]{2,1,0:T(8,128)(2,1)S(1)}, u32[]{:S(2)}, u32[]{:S(2)}) collective-permute-start(bf16[4,32,128]{2,1,0:T(8,128)(2,1)S(1)} %get-tuple-element.13), channel_id=1, source_target_pairs={{0,3},{1,2},{2,1},{3,0},{4,7},{5,6},{6,5},{7,4},{8,11},{9,10},{10,... | collective-permute-start | bytes 98312 | tf_op jit(solution)/shard_map/ppermute | solution.py:193
  12.1 0.5 %collective-permute-start.5 = (bf16[4,32,128]{2,1,0:T(8,128)(2,1)S(1)}, bf16[4,32,128]{2,1,0:T(8,128)(2,1)S(1)}, u32[]{:S(2)}, u32[]{:S(2)}) collective-permute-start(bf16[4,32,128]{2,1,0:T(8,128)(2,1)S(1)} %get-tuple-element.13), channel_id=1, source_target_pairs={{0,2},{1,3},{2,0},{3,1},{4,6},{5,7},{6,4},{7,5},{8,10},{9,11},{10,... | collective-permute-start | bytes 98312 | tf_op jit(solution)/shard_map/ppermute | solution.py:193
  12.7 1.4 %shard_map.61.refs_0_ = f32[8,64]{1,0:T(8,128)S(1)} custom-call(bf16[8192,128]{1,0:T(8,128)(2,1)S(1)} %shard_map.59.tokens_ref.refs_3_, bf16[256,128]{1,0:T(8,128)(2,1)S(1)} %bitcast.10), custom_call_target="tpu_custom_call" | custom-call | flops 1073741824 | bytes 4194304 | tf_op jit(solution)/shard_map/pallas_call | solution.py:148
  14.1 0.9 %shard_map.60.refs_2_.after_ref = f32[4,64]{1,0:T(4,128)S(1)} custom-call(bf16[8192,128]{1,0:T(8,128)(2,1)S(1)} %shard_map.59.tokens_ref.refs_3_, bf16[128,128]{1,0:T(8,128)(2,1)S(1)} %bitcast.6), custom_call_target="tpu_custom_call" | custom-call | flops 536870912 | bytes 4194304 | tf_op jit(solution)/shard_map/pallas_call | solution.py:148
  14.9 1.1 %collective-permute-done.5 = bf16[4,32,128]{2,1,0:T(8,128)(2,1)S(1)} collective-permute-done((bf16[4,32,128]{2,1,0:T(8,128)(2,1)S(1)}, bf16[4,32,128]{2,1,0:T(8,128)(2,1)S(1)}, u32[]{:S(2)}, u32[]{:S(2)}) %collective-permute-start.5) | collective-permute-done | bytes 32800 | tf_op jit(solution)/shard_map/ppermute | solution.py:193
  16.1 0.8 %shard_map.62.refs_1_ = f32[4,64]{1,0:T(4,128)S(1)} custom-call(bf16[8192,128]{1,0:T(8,128)(2,1)S(1)} %shard_map.59.tokens_ref.refs_3_, bf16[128,128]{1,0:T(8,128)(2,1)S(1)} %bitcast.7), custom_call_target="tpu_custom_call" | custom-call | flops 536870912 | bytes 4194304 | tf_op jit(solution)/shard_map/pallas_call | solution.py:148
  16.9 0.4 %collective-permute-start.8 = (f32[4,64]{1,0:T(4,128)S(1)}, f32[4,64]{1,0:T(4,128)S(1)}, u32[]{:S(2)}, u32[]{:S(2)}) collective-permute-start(f32[4,64]{1,0:T(4,128)S(1)} %shard_map.60.refs_2_.after_ref), channel_id=1, source_target_pairs={{0,3},{1,2},{2,1},{3,0},{4,7},{5,6},{6,5},{7,4},{8,11},{9,10},{10,... | collective-permute-start | bytes 3080 | tf_op jit(solution)/shard_map/ppermute | solution.py:193
  17.3 0.4 %collective-permute-start.7 = (f32[4,64]{1,0:T(4,128)S(1)}, f32[4,64]{1,0:T(4,128)S(1)}, u32[]{:S(2)}, u32[]{:S(2)}) collective-permute-start(f32[4,64]{1,0:T(4,128)S(1)} %shard_map.62.refs_1_), channel_id=1, source_target_pairs={{0,2},{1,3},{2,0},{3,1},{4,6},{5,7},{6,4},{7,5},{8,10},{9,11},{10,... | collective-permute-start | bytes 3080 | tf_op jit(solution)/shard_map/ppermute | solution.py:193
  17.7 1.2 %shard_map.63.tokens_ref = bf16[8192,64]{1,0:T(8,128)(2,1)S(1)} custom-call(f32[8,64]{1,0:T(8,128)S(1)} %shard_map.61.refs_0_, f32[4,64]{1,0:T(4,128)S(1)} %shard_map.62.refs_1_, f32[4,64]{1,0:T(4,128)S(1)} %shard_map.60.refs_2_.after_ref, bf16[8192,128]{1,0:T(8,128)(2,1)S(1)} %shard_map.59.tokens_ref.refs_3_), custom_call_target="tpu_custom_call" | custom-call | flops 8388608 | bytes 4194304 | tf_op jit(solution)/shard_map/pallas_call | solution.py:73
  18.9 1.1 %collective-permute-start.6 = (f32[4,64]{1,0:T(4,128)S(1)}, f32[4,64]{1,0:T(4,128)S(1)}, u32[]{:S(2)}, u32[]{:S(2)}) collective-permute-start(f32[4,64]{1,0:T(4,128)S(1)} %get-tuple-element.25), channel_id=1, source_target_pairs={{0,1},{1,0},{2,3},{3,2},{4,5},{5,4},{6,7},{7,6},{8,9},{9,8},{10,11... | collective-permute-start | bytes 3080 | tf_op jit(solution)/shard_map/ppermute | solution.py:193
  20.1 0.9 %shard_map.64.rest_0_ = f32[16,64]{1,0:T(8,128)S(1)} custom-call(f32[4,64]{1,0:T(4,128)S(1)} %shard_map.60.refs_2_.after_ref, bf16[8192,64]{1,0:T(8,128)(2,1)S(1)} %shard_map.63.tokens_ref, bf16[128,128]{1,0:T(8,128)(2,1)S(1)} %bitcast.9), custom_call_target="tpu_custom_call" | custom-call | flops 536870912 | bytes 4194304 | tf_op jit(solution)/shard_map/pallas_call | solution.py:148
  21.0 0.1 pad_maximum_fusion.1
  21.1 2.0 %collective-permute-start.11 = (f32[1,256]{1,0:T(1,128)S(1)}, f32[1,256]{1,0:T(1,128)S(1)}, u32[]{:S(2)}, u32[]{:S(2)}) collective-permute-start(f32[1,256]{1,0:T(1,128)S(1)} %get-tuple-element.21), channel_id=1, source_target_pairs={{0,12},{1,13},{2,14},{3,15},{4,8},{5,9},{6,10},{7,11},{8,4},{9,5},... | collective-permute-start | bytes 3080 | tf_op jit(solution)/shard_map/ppermute | solution.py:193
  23.2 0.2 collective-permute-start.10
  23.4 2.1 %collective-permute-start.9 = (f32[1,256]{1,0:T(1,128)S(1)}, f32[1,256]{1,0:T(1,128)S(1)}, u32[]{:S(2)}, u32[]{:S(2)}) collective-permute-start(f32[1,256]{1,0:T(1,128)S(1)} %get-tuple-element.23), channel_id=1, source_target_pairs={{0,4},{1,5},{2,6},{3,7},{4,0},{5,1},{6,2},{7,3},{8,12},{9,13},{10,... | collective-permute-start | bytes 3080 | tf_op jit(solution)/shard_map/ppermute | solution.py:193
  25.6 2.0 %shard_map.65.coarse_ref = f32[16,64]{1,0:T(8,128)S(1)} custom-call(f32[4,64]{1,0:T(4,128)S(1)} %shard_map.60.refs_2_.after_ref, bf16[8192,64]{1,0:T(8,128)(2,1)S(1)} %shard_map.63.tokens_ref, bf16[384,128]{1,0:T(8,128)(2,1)S(1)} %bitcast.8, f32[16,64]{1,0:T(8,128)S(1)} %shard_map.64.rest_0_), custom_call_target="tpu_custom_call" | custom-call | flops 1610612736 | bytes 4194304 | tf_op jit(solution)/shard_map/pallas_call | solution.py:148
  27.7 0.7 %shard_map.66 = (f32[1,96]{1,0:T(1,128)}, f32[16,64]{1,0:T(8,128)}) custom-call(f32[16,64]{1,0:T(8,128)S(1)} %shard_map.65.coarse_ref, s32[1,96]{1,0:T(1,128)S(1)} %copy-done.1, f32[1,1024]{1,0:T(1,128)S(1)} %pad_maximum_fusion.2.returned_ref), custom_call_target="tpu_custom_call" | custom-call | tf_op jit(solution)/shard_map/pallas_call | solution.py:239
  (22 shorter events, 0.2 us)
Async XLA Ops:
  0.6 8.7 %collective-permute-start = (bf16[1,32,128]{2,1,0:T(8,128)(2,1)}, bf16[1,32,128]{2,1,0:T(8,128)(2,1)S(1)}, u32[]{:S(2)}, u32[]{:S(2)}) collective-permute-start(bf16[1,32,128]{2,1,0:T(8,128)(2,1)} %param.4), channel_id=1, source_target_pairs={{0,8},{1,9},{2,10},{3,11},{4,12},{5,13},{6,14},{7,15},{8,0},{9,1},... | collective-permute-start | bytes 24584 | tf_op jit(solution)/shard_map/ppermute | solution.py:193
  4.7 5.7 %collective-permute-start.1 = (bf16[1,32,128]{2,1,0:T(8,128)(2,1)}, bf16[1,32,128]{2,1,0:T(8,128)(2,1)S(1)}, u32[]{:S(2)}, u32[]{:S(2)}) collective-permute-start(bf16[1,32,128]{2,1,0:T(8,128)(2,1)} %param.4), channel_id=1, source_target_pairs={{0,12},{1,13},{2,14},{3,15},{4,8},{5,9},{6,10},{7,11},{8,4},{9,5},... | collective-permute-start | bytes 24584 | tf_op jit(solution)/shard_map/ppermute | solution.py:193
  6.1 4.3 %collective-permute-start.2 = (bf16[1,32,128]{2,1,0:T(8,128)(2,1)}, bf16[1,32,128]{2,1,0:T(8,128)(2,1)S(1)}, u32[]{:S(2)}, u32[]{:S(2)}) collective-permute-start(bf16[1,32,128]{2,1,0:T(8,128)(2,1)} %param.4), channel_id=1, source_target_pairs={{0,4},{1,5},{2,6},{3,7},{4,0},{5,1},{6,2},{7,3},{8,12},{9,13},{10,... | collective-permute-start | bytes 24584 | tf_op jit(solution)/shard_map/ppermute | solution.py:193
  7.0 0.7 %copy-start = (s32[64]{0:T(128)S(1)}, s32[64]{0:T(128)}, u32[]{:S(2)}) copy-start(s32[64]{0:T(128)} %lens_hbm.1) | copy-start | bytes 772
  10.4 2.2 %collective-permute-start.4 = (bf16[4,32,128]{2,1,0:T(8,128)(2,1)S(1)}, bf16[4,32,128]{2,1,0:T(8,128)(2,1)S(1)}, u32[]{:S(2)}, u32[]{:S(2)}) collective-permute-start(bf16[4,32,128]{2,1,0:T(8,128)(2,1)S(1)} %get-tuple-element.13), channel_id=1, source_target_pairs={{0,1},{1,0},{2,3},{3,2},{4,5},{5,4},{6,7},{7,6},{8,9},{9,8},{10,11... | collective-permute-start | bytes 98312 | tf_op jit(solution)/shard_map/ppermute | solution.py:193
  10.5 3.5 %collective-permute-start.3 = (bf16[4,32,128]{2,1,0:T(8,128)(2,1)S(1)}, bf16[4,32,128]{2,1,0:T(8,128)(2,1)S(1)}, u32[]{:S(2)}, u32[]{:S(2)}) collective-permute-start(bf16[4,32,128]{2,1,0:T(8,128)(2,1)S(1)} %get-tuple-element.13), channel_id=1, source_target_pairs={{0,3},{1,2},{2,1},{3,0},{4,7},{5,6},{6,5},{7,4},{8,11},{9,10},{10,... | collective-permute-start | bytes 98312 | tf_op jit(solution)/shard_map/ppermute | solution.py:193
  12.1 3.9 %collective-permute-start.5 = (bf16[4,32,128]{2,1,0:T(8,128)(2,1)S(1)}, bf16[4,32,128]{2,1,0:T(8,128)(2,1)S(1)}, u32[]{:S(2)}, u32[]{:S(2)}) collective-permute-start(bf16[4,32,128]{2,1,0:T(8,128)(2,1)S(1)} %get-tuple-element.13), channel_id=1, source_target_pairs={{0,2},{1,3},{2,0},{3,1},{4,6},{5,7},{6,4},{7,5},{8,10},{9,11},{10,... | collective-permute-start | bytes 98312 | tf_op jit(solution)/shard_map/ppermute | solution.py:193
  16.9 4.1 %collective-permute-start.8 = (f32[4,64]{1,0:T(4,128)S(1)}, f32[4,64]{1,0:T(4,128)S(1)}, u32[]{:S(2)}, u32[]{:S(2)}) collective-permute-start(f32[4,64]{1,0:T(4,128)S(1)} %shard_map.60.refs_2_.after_ref), channel_id=1, source_target_pairs={{0,3},{1,2},{2,1},{3,0},{4,7},{5,6},{6,5},{7,4},{8,11},{9,10},{10,... | collective-permute-start | bytes 3080 | tf_op jit(solution)/shard_map/ppermute | solution.py:193
  17.3 3.7 %collective-permute-start.7 = (f32[4,64]{1,0:T(4,128)S(1)}, f32[4,64]{1,0:T(4,128)S(1)}, u32[]{:S(2)}, u32[]{:S(2)}) collective-permute-start(f32[4,64]{1,0:T(4,128)S(1)} %shard_map.62.refs_1_), channel_id=1, source_target_pairs={{0,2},{1,3},{2,0},{3,1},{4,6},{5,7},{6,4},{7,5},{8,10},{9,11},{10,... | collective-permute-start | bytes 3080 | tf_op jit(solution)/shard_map/ppermute | solution.py:193
  18.9 2.1 %collective-permute-start.6 = (f32[4,64]{1,0:T(4,128)S(1)}, f32[4,64]{1,0:T(4,128)S(1)}, u32[]{:S(2)}, u32[]{:S(2)}) collective-permute-start(f32[4,64]{1,0:T(4,128)S(1)} %get-tuple-element.25), channel_id=1, source_target_pairs={{0,1},{1,0},{2,3},{3,2},{4,5},{5,4},{6,7},{7,6},{8,9},{9,8},{10,11... | collective-permute-start | bytes 3080 | tf_op jit(solution)/shard_map/ppermute | solution.py:193
  21.1 6.5 %collective-permute-start.11 = (f32[1,256]{1,0:T(1,128)S(1)}, f32[1,256]{1,0:T(1,128)S(1)}, u32[]{:S(2)}, u32[]{:S(2)}) collective-permute-start(f32[1,256]{1,0:T(1,128)S(1)} %get-tuple-element.21), channel_id=1, source_target_pairs={{0,12},{1,13},{2,14},{3,15},{4,8},{5,9},{6,10},{7,11},{8,4},{9,5},... | collective-permute-start | bytes 3080 | tf_op jit(solution)/shard_map/ppermute | solution.py:193
  23.2 4.5 %collective-permute-start.10 = (f32[1,256]{1,0:T(1,128)S(1)}, f32[1,256]{1,0:T(1,128)S(1)}, u32[]{:S(2)}, u32[]{:S(2)}) collective-permute-start(f32[1,256]{1,0:T(1,128)S(1)} %get-tuple-element.22), channel_id=1, source_target_pairs={{0,8},{1,9},{2,10},{3,11},{4,12},{5,13},{6,14},{7,15},{8,0},{9,1},... | collective-permute-start | bytes 3080 | tf_op jit(solution)/shard_map/ppermute | solution.py:193
  23.4 4.2 %collective-permute-start.9 = (f32[1,256]{1,0:T(1,128)S(1)}, f32[1,256]{1,0:T(1,128)S(1)}, u32[]{:S(2)}, u32[]{:S(2)}) collective-permute-start(f32[1,256]{1,0:T(1,128)S(1)} %get-tuple-element.23), channel_id=1, source_target_pairs={{0,4},{1,5},{2,6},{3,7},{4,0},{5,1},{6,2},{7,3},{8,12},{9,13},{10,... | collective-permute-start | bytes 3080 | tf_op jit(solution)/shard_map/ppermute | solution.py:193
  25.6 2.1 %copy-start.1 = (s32[1,96]{1,0:T(1,128)S(1)}, s32[1,96]{1,0:T(1,128)}, u32[]{:S(2)}) copy-start(s32[1,96]{1,0:T(1,128)} %ids_ref.1) | copy-start | bytes 1156

commit v6 on v5

--- a/solution.py
+++ b/solution.py
@@ -130,7 +130,8 @@
     out_ref[...] = average(best_ref, 0, places, places)
 
 
-def coarse_kernel(order, first, places, after_ref, tokens_ref, queries_ref, *rest):
+def coarse_kernel(order, first, places, *refs):
+    tokens_ref, queries_ref, *rest = refs if first else refs[1:]
     out_ref, best_ref = rest[-2:]
     count, width = best_ref.shape[0], tokens_ref.shape[0] // best_ref.shape[0]
     maxima(tokens_ref, unit_prefix(queries_ref[...].astype(jnp.float32)), best_ref, count, width)
@@ -235,7 +236,7 @@
             near_kernel = functools.partial(coarse_kernel, order, 0, held.shape[0])
             far_kernel = functools.partial(coarse_kernel, order, held.shape[0], owners - held.shape[0])
             coarse = score(near_kernel, owners, count, prefix, held, after=(scores[-1],))
-            coarse = score(far_kernel, owners, count, prefix, join(*came), after=(scores[-1],), partial=(coarse,))
+            coarse = score(far_kernel, owners, count, prefix, join(*came), partial=(coarse,))
     exact, coarse = pl.pallas_call(
         functools.partial(pick_kernel, count, order),
         out_shape=(

time: 28.6 us -> 28.2 us (0.986)
  starting transfers between devices: 14.3 us -> 14 us
    unnamed x8 -> x7, local copies, waits for them, and re-layouts: 1.42 us -> 1.41 us
  transfers between devices with their start and end apart: 12 -> 12, of which waited for: 2 -> 4; matrix products, arithmetic and copies ran while one was open for 3% -> 3% of each run, Pallas kernels for 28% -> 29%
where the time goes in v6:
time: 28.2 us; the launch traced here: 27.9 us
  starting transfers between devices  14 us (50%)
  Pallas kernels  9.57 us (34%)
  waiting for transfers between devices  2.12 us (8%)
  local copies, waits for them, and re-layouts  1.44 us (5%)
  between operations  0.71 us (3%)
    ppermute x12, starting transfers between devices, exchange(): return lax.ppermute(array, 'slab', [(i, i ^ offset) for i in range(owners)])  14 us
    pallas_call x5, Pallas kernels, score(): pl.pallas_call(kernel, out_shape=jax.ShapeDtypeStruct((rows, count), jnp....  6.03 us
    ppermute x12, waiting for transfers between devices, exchange(): return lax.ppermute(array, 'slab', [(i, i ^ offset) for i in range(owners)])  2.12 us
    pallas_call x1, Pallas kernels, live_tokens(): pl.pallas_call(live_kernel, out_shape=jax.ShapeDtypeStruct((count * width...  1.64 us
    unnamed x7, local copies, waits for them, and re-layouts  1.41 us
    pallas_call x1, Pallas kernels, prefixes(): pl.pallas_call(prefix_kernel, out_shape=jax.ShapeDtypeStruct((full.shape[...  1.18 us
    pallas_call x1, Pallas kernels, per_device(): pl.pallas_call(functools.partial(pick_kernel, count, order), out_shape=(j...  0.72 us
  transfers between devices with their start and end apart: 12, of which 4 were waited for; matrix products, arithmetic and copies ran while one was open for 3% of the time, Pallas kernels for 29%

profile of v6, /device:TPU:0, one launch (start us, length us, event | category | flops | bytes accessed | tf_op | source)
XLA Modules:
  0.0 27.9 jit_solution(13134159980898472012)
XLA Ops:
  0.6 4.1 %collective-permute-start = (bf16[1,32,128]{2,1,0:T(8,128)(2,1)}, bf16[1,32,128]{2,1,0:T(8,128)(2,1)S(1)}, u32[]{:S(2)}, u32[]{:S(2)}) collective-permute-start(bf16[1,32,128]{2,1,0:T(8,128)(2,1)} %param.4), channel_id=1, source_target_pairs={{0,8},{1,9},{2,10},{3,11},{4,12},{5,13},{6,14},{7,15},{8,0},{9,1},... | collective-permute-start | bytes 24584 | tf_op jit(solution)/shard_map/ppermute | solution.py:194
  4.7 1.3 %collective-permute-start.1 = (bf16[1,32,128]{2,1,0:T(8,128)(2,1)}, bf16[1,32,128]{2,1,0:T(8,128)(2,1)S(1)}, u32[]{:S(2)}, u32[]{:S(2)}) collective-permute-start(bf16[1,32,128]{2,1,0:T(8,128)(2,1)} %param.4), channel_id=1, source_target_pairs={{0,12},{1,13},{2,14},{3,15},{4,8},{5,9},{6,10},{7,11},{8,4},{9,5},... | collective-permute-start | bytes 24584 | tf_op jit(solution)/shard_map/ppermute | solution.py:194
  6.1 0.2 collective-permute-start.2
  6.3 0.7 %constant_dynamic-update-slice_fusion.3 = (bf16[4,32,128]{2,1,0:T(8,128)(2,1)S(1)}, bf16[8,32,128]{2,1,0:T(8,128)(2,1)S(1)}) fusion(bf16[1,32,128]{2,1,0:T(8,128)(2,1)} %param.4), kind=kLoop, calls=%fused_computation.4 | loop fusion | bytes 24576
  7.0 0.7 %copy-done = s32[64]{0:T(128)S(1)} copy-done((s32[64]{0:T(128)S(1)}, s32[64]{0:T(128)}, u32[]{:S(2)}) %copy-start) | copy-done | bytes 280
  7.7 1.6 %shard_map.59.tokens_ref.refs_3_ = bf16[8192,128]{1,0:T(8,128)(2,1)S(1)} custom-call(s32[64]{0:T(128)S(1)} %copy-done, bf16[64,128,128]{2,1,0:T(8,128)(2,1)} %passages_hbm.1), custom_call_target="tpu_custom_call" | custom-call | flops 8388608 | bytes 6291456 | tf_op jit(solution)/shard_map/pallas_call | solution.py:50
  9.4 1.0 %collective-permute-done.1 = bf16[1,32,128]{2,1,0:T(8,128)(2,1)S(1)} collective-permute-done((bf16[1,32,128]{2,1,0:T(8,128)(2,1)}, bf16[1,32,128]{2,1,0:T(8,128)(2,1)S(1)}, u32[]{:S(2)}, u32[]{:S(2)}) %collective-permute-start.1) | collective-permute-done | bytes 8224 | tf_op jit(solution)/shard_map/ppermute | solution.py:194
  10.5 1.6 %collective-permute-start.4 = (bf16[4,32,128]{2,1,0:T(8,128)(2,1)S(1)}, bf16[4,32,128]{2,1,0:T(8,128)(2,1)S(1)}, u32[]{:S(2)}, u32[]{:S(2)}) collective-permute-start(bf16[4,32,128]{2,1,0:T(8,128)(2,1)S(1)} %get-tuple-element.12), channel_id=1, source_target_pairs={{0,2},{1,3},{2,0},{3,1},{4,6},{5,7},{6,4},{7,5},{8,10},{9,11},{10,... | collective-permute-start | bytes 98312 | tf_op jit(solution)/shard_map/ppermute | solution.py:194
  12.1 0.3 collective-permute-start.5
  12.4 1.4 %shard_map.60.refs_0_ = f32[8,64]{1,0:T(8,128)S(1)} custom-call(bf16[8192,128]{1,0:T(8,128)(2,1)S(1)} %shard_map.59.tokens_ref.refs_3_, bf16[256,128]{1,0:T(8,128)(2,1)S(1)} %bitcast.10), custom_call_target="tpu_custom_call" | custom-call | flops 1073741824 | bytes 4194304 | tf_op jit(solution)/shard_map/pallas_call | solution.py:149
  13.8 0.7 %collective-permute-done.4 = bf16[4,32,128]{2,1,0:T(8,128)(2,1)S(1)} collective-permute-done((bf16[4,32,128]{2,1,0:T(8,128)(2,1)S(1)}, bf16[4,32,128]{2,1,0:T(8,128)(2,1)S(1)}, u32[]{:S(2)}, u32[]{:S(2)}) %collective-permute-start.4) | collective-permute-done | bytes 32800 | tf_op jit(solution)/shard_map/ppermute | solution.py:194
  14.5 0.8 %shard_map.61.refs_1_ = f32[4,64]{1,0:T(4,128)S(1)} custom-call(bf16[8192,128]{1,0:T(8,128)(2,1)S(1)} %shard_map.59.tokens_ref.refs_3_, bf16[128,128]{1,0:T(8,128)(2,1)S(1)} %bitcast.6), custom_call_target="tpu_custom_call" | custom-call | flops 536870912 | bytes 4194304 | tf_op jit(solution)/shard_map/pallas_call | solution.py:149
  15.4 0.8 %shard_map.62.refs_2_.refs_0_ = f32[4,64]{1,0:T(4,128)S(1)} custom-call(bf16[8192,128]{1,0:T(8,128)(2,1)S(1)} %shard_map.59.tokens_ref.refs_3_, bf16[128,128]{1,0:T(8,128)(2,1)S(1)} %bitcast.7), custom_call_target="tpu_custom_call" | custom-call | flops 536870912 | bytes 4194304 | tf_op jit(solution)/shard_map/pallas_call | solution.py:149
  16.3 0.7 %collective-permute-start.8 = (f32[4,64]{1,0:T(4,128)S(1)}, f32[4,64]{1,0:T(4,128)S(1)}, u32[]{:S(2)}, u32[]{:S(2)}) collective-permute-start(f32[4,64]{1,0:T(4,128)S(1)} %shard_map.62.refs_2_.refs_0_), channel_id=1, source_target_pairs={{0,3},{1,2},{2,1},{3,0},{4,7},{5,6},{6,5},{7,4},{8,11},{9,10},{10,... | collective-permute-start | bytes 3080 | tf_op jit(solution)/shard_map/ppermute | solution.py:194
  17.0 1.1 %collective-permute-start.7 = (f32[4,64]{1,0:T(4,128)S(1)}, f32[4,64]{1,0:T(4,128)S(1)}, u32[]{:S(2)}, u32[]{:S(2)}) collective-permute-start(f32[4,64]{1,0:T(4,128)S(1)} %shard_map.61.refs_1_), channel_id=1, source_target_pairs={{0,2},{1,3},{2,0},{3,1},{4,6},{5,7},{6,4},{7,5},{8,10},{9,11},{10,... | collective-permute-start | bytes 3080 | tf_op jit(solution)/shard_map/ppermute | solution.py:194
  18.1 1.2 %shard_map.63.refs_1_.refs_0_ = bf16[8192,64]{1,0:T(8,128)(2,1)S(1)} custom-call(f32[8,64]{1,0:T(8,128)S(1)} %shard_map.60.refs_0_, f32[4,64]{1,0:T(4,128)S(1)} %shard_map.61.refs_1_, f32[4,64]{1,0:T(4,128)S(1)} %shard_map.62.refs_2_.refs_0_, bf16[8192,128]{1,0:T(8,128)(2,1)S(1)} %shard_map.59.tokens_ref.refs_3_), custom_call_target="tpu_custom_call" | custom-call | flops 8388608 | bytes 4194304 | tf_op jit(solution)/shard_map/pallas_call | solution.py:73
  19.3 0.1 collective-permute-start.6
  19.5 0.9 %shard_map.64.refs_2_ = f32[16,64]{1,0:T(8,128)S(1)} custom-call(f32[4,64]{1,0:T(4,128)S(1)} %shard_map.62.refs_2_.refs_0_, bf16[8192,64]{1,0:T(8,128)(2,1)S(1)} %shard_map.63.refs_1_.refs_0_, bf16[128,128]{1,0:T(8,128)(2,1)S(1)} %bitcast.9), custom_call_target="tpu_custom_call" | custom-call | flops 536870912 | bytes 4194304 | tf_op jit(solution)/shard_map/pallas_call | solution.py:149
  20.4 0.2 collective-permute-done.7
  20.7 2.0 %collective-permute-start.11 = (f32[1,256]{1,0:T(1,128)S(1)}, f32[1,256]{1,0:T(1,128)S(1)}, u32[]{:S(2)}, u32[]{:S(2)}) collective-permute-start(f32[1,256]{1,0:T(1,128)S(1)} %get-tuple-element.21), channel_id=1, source_target_pairs={{0,12},{1,13},{2,14},{3,15},{4,8},{5,9},{6,10},{7,11},{8,4},{9,5},... | collective-permute-start | bytes 3080 | tf_op jit(solution)/shard_map/ppermute | solution.py:194
  22.7 0.2 collective-permute-start.10
  23.0 2.1 %collective-permute-start.9 = (f32[1,256]{1,0:T(1,128)S(1)}, f32[1,256]{1,0:T(1,128)S(1)}, u32[]{:S(2)}, u32[]{:S(2)}) collective-permute-start(f32[1,256]{1,0:T(1,128)S(1)} %get-tuple-element.23), channel_id=1, source_target_pairs={{0,4},{1,5},{2,6},{3,7},{4,0},{5,1},{6,2},{7,3},{8,12},{9,13},{10,... | collective-permute-start | bytes 3080 | tf_op jit(solution)/shard_map/ppermute | solution.py:194
  25.1 2.0 %shard_map.65.coarse_ref = f32[16,64]{1,0:T(8,128)S(1)} custom-call(bf16[8192,64]{1,0:T(8,128)(2,1)S(1)} %shard_map.63.refs_1_.refs_0_, bf16[384,128]{1,0:T(8,128)(2,1)S(1)} %bitcast.8, f32[16,64]{1,0:T(8,128)S(1)} %shard_map.64.refs_2_), custom_call_target="tpu_custom_call" | custom-call | flops 1610612736 | bytes 4194304 | tf_op jit(solution)/shard_map/pallas_call | solution.py:149
  27.2 0.7 %shard_map.66 = (f32[1,96]{1,0:T(1,128)}, f32[16,64]{1,0:T(8,128)}) custom-call(f32[16,64]{1,0:T(8,128)S(1)} %shard_map.65.coarse_ref, s32[1,96]{1,0:T(1,128)S(1)} %copy-done.1, f32[1,1024]{1,0:T(1,128)S(1)} %pad_maximum_fusion.2.returned_ref), custom_call_target="tpu_custom_call" | custom-call | tf_op jit(solution)/shard_map/pallas_call | solution.py:240
  (22 shorter events, 0.4 us)
Async XLA Ops:
  0.6 8.7 %collective-permute-start = (bf16[1,32,128]{2,1,0:T(8,128)(2,1)}, bf16[1,32,128]{2,1,0:T(8,128)(2,1)S(1)}, u32[]{:S(2)}, u32[]{:S(2)}) collective-permute-start(bf16[1,32,128]{2,1,0:T(8,128)(2,1)} %param.4), channel_id=1, source_target_pairs={{0,8},{1,9},{2,10},{3,11},{4,12},{5,13},{6,14},{7,15},{8,0},{9,1},... | collective-permute-start | bytes 24584 | tf_op jit(solution)/shard_map/ppermute | solution.py:194
  4.7 5.7 %collective-permute-start.1 = (bf16[1,32,128]{2,1,0:T(8,128)(2,1)}, bf16[1,32,128]{2,1,0:T(8,128)(2,1)S(1)}, u32[]{:S(2)}, u32[]{:S(2)}) collective-permute-start(bf16[1,32,128]{2,1,0:T(8,128)(2,1)} %param.4), channel_id=1, source_target_pairs={{0,12},{1,13},{2,14},{3,15},{4,8},{5,9},{6,10},{7,11},{8,4},{9,5},... | collective-permute-start | bytes 24584 | tf_op jit(solution)/shard_map/ppermute | solution.py:194
  6.1 4.3 %collective-permute-start.2 = (bf16[1,32,128]{2,1,0:T(8,128)(2,1)}, bf16[1,32,128]{2,1,0:T(8,128)(2,1)S(1)}, u32[]{:S(2)}, u32[]{:S(2)}) collective-permute-start(bf16[1,32,128]{2,1,0:T(8,128)(2,1)} %param.4), channel_id=1, source_target_pairs={{0,4},{1,5},{2,6},{3,7},{4,0},{5,1},{6,2},{7,3},{8,12},{9,13},{10,... | collective-permute-start | bytes 24584 | tf_op jit(solution)/shard_map/ppermute | solution.py:194
  7.0 0.7 %copy-start = (s32[64]{0:T(128)S(1)}, s32[64]{0:T(128)}, u32[]{:S(2)}) copy-start(s32[64]{0:T(128)} %lens_hbm.1) | copy-start | bytes 772
  10.4 1.9 %collective-permute-start.3 = (bf16[4,32,128]{2,1,0:T(8,128)(2,1)S(1)}, bf16[4,32,128]{2,1,0:T(8,128)(2,1)S(1)}, u32[]{:S(2)}, u32[]{:S(2)}) collective-permute-start(bf16[4,32,128]{2,1,0:T(8,128)(2,1)S(1)} %get-tuple-element.12), channel_id=1, source_target_pairs={{0,1},{1,0},{2,3},{3,2},{4,5},{5,4},{6,7},{7,6},{8,9},{9,8},{10,11... | collective-permute-start | bytes 98312 | tf_op jit(solution)/shard_map/ppermute | solution.py:194
  10.5 4.0 %collective-permute-start.4 = (bf16[4,32,128]{2,1,0:T(8,128)(2,1)S(1)}, bf16[4,32,128]{2,1,0:T(8,128)(2,1)S(1)}, u32[]{:S(2)}, u32[]{:S(2)}) collective-permute-start(bf16[4,32,128]{2,1,0:T(8,128)(2,1)S(1)} %get-tuple-element.12), channel_id=1, source_target_pairs={{0,2},{1,3},{2,0},{3,1},{4,6},{5,7},{6,4},{7,5},{8,10},{9,11},{10,... | collective-permute-start | bytes 98312 | tf_op jit(solution)/shard_map/ppermute | solution.py:194
  12.1 3.3 %collective-permute-start.5 = (bf16[4,32,128]{2,1,0:T(8,128)(2,1)S(1)}, bf16[4,32,128]{2,1,0:T(8,128)(2,1)S(1)}, u32[]{:S(2)}, u32[]{:S(2)}) collective-permute-start(bf16[4,32,128]{2,1,0:T(8,128)(2,1)S(1)} %get-tuple-element.12), channel_id=1, source_target_pairs={{0,3},{1,2},{2,1},{3,0},{4,7},{5,6},{6,5},{7,4},{8,11},{9,10},{10,... | collective-permute-start | bytes 98312 | tf_op jit(solution)/shard_map/ppermute | solution.py:194
  16.3 4.1 %collective-permute-start.8 = (f32[4,64]{1,0:T(4,128)S(1)}, f32[4,64]{1,0:T(4,128)S(1)}, u32[]{:S(2)}, u32[]{:S(2)}) collective-permute-start(f32[4,64]{1,0:T(4,128)S(1)} %shard_map.62.refs_2_.refs_0_), channel_id=1, source_target_pairs={{0,3},{1,2},{2,1},{3,0},{4,7},{5,6},{6,5},{7,4},{8,11},{9,10},{10,... | collective-permute-start | bytes 3080 | tf_op jit(solution)/shard_map/ppermute | solution.py:194
  17.0 3.6 %collective-permute-start.7 = (f32[4,64]{1,0:T(4,128)S(1)}, f32[4,64]{1,0:T(4,128)S(1)}, u32[]{:S(2)}, u32[]{:S(2)}) collective-permute-start(f32[4,64]{1,0:T(4,128)S(1)} %shard_map.61.refs_1_), channel_id=1, source_target_pairs={{0,2},{1,3},{2,0},{3,1},{4,6},{5,7},{6,4},{7,5},{8,10},{9,11},{10,... | collective-permute-start | bytes 3080 | tf_op jit(solution)/shard_map/ppermute | solution.py:194
  19.3 1.3 %collective-permute-start.6 = (f32[4,64]{1,0:T(4,128)S(1)}, f32[4,64]{1,0:T(4,128)S(1)}, u32[]{:S(2)}, u32[]{:S(2)}) collective-permute-start(f32[4,64]{1,0:T(4,128)S(1)} %get-tuple-element.25), channel_id=1, source_target_pairs={{0,1},{1,0},{2,3},{3,2},{4,5},{5,4},{6,7},{7,6},{8,9},{9,8},{10,11... | collective-permute-start | bytes 3080 | tf_op jit(solution)/shard_map/ppermute | solution.py:194
  20.7 6.5 %collective-permute-start.11 = (f32[1,256]{1,0:T(1,128)S(1)}, f32[1,256]{1,0:T(1,128)S(1)}, u32[]{:S(2)}, u32[]{:S(2)}) collective-permute-start(f32[1,256]{1,0:T(1,128)S(1)} %get-tuple-element.21), channel_id=1, source_target_pairs={{0,12},{1,13},{2,14},{3,15},{4,8},{5,9},{6,10},{7,11},{8,4},{9,5},... | collective-permute-start | bytes 3080 | tf_op jit(solution)/shard_map/ppermute | solution.py:194
  22.7 4.5 %collective-permute-start.10 = (f32[1,256]{1,0:T(1,128)S(1)}, f32[1,256]{1,0:T(1,128)S(1)}, u32[]{:S(2)}, u32[]{:S(2)}) collective-permute-start(f32[1,256]{1,0:T(1,128)S(1)} %get-tuple-element.22), channel_id=1, source_target_pairs={{0,8},{1,9},{2,10},{3,11},{4,12},{5,13},{6,14},{7,15},{8,0},{9,1},... | collective-permute-start | bytes 3080 | tf_op jit(solution)/shard_map/ppermute | solution.py:194
  23.0 4.2 %collective-permute-start.9 = (f32[1,256]{1,0:T(1,128)S(1)}, f32[1,256]{1,0:T(1,128)S(1)}, u32[]{:S(2)}, u32[]{:S(2)}) collective-permute-start(f32[1,256]{1,0:T(1,128)S(1)} %get-tuple-element.23), channel_id=1, source_target_pairs={{0,4},{1,5},{2,6},{3,7},{4,0},{5,1},{6,2},{7,3},{8,12},{9,13},{10,... | collective-permute-start | bytes 3080 | tf_op jit(solution)/shard_map/ppermute | solution.py:194
  25.1 2.1 %copy-start.1 = (s32[1,96]{1,0:T(1,128)S(1)}, s32[1,96]{1,0:T(1,128)}, u32[]{:S(2)}) copy-start(s32[1,96]{1,0:T(1,128)} %ids_ref.1) | copy-start | bytes 1156

commit v7 on v5

--- a/solution.py
+++ b/solution.py
@@ -62,32 +62,18 @@
     )(lengths, passages)
 
 
-def prefix_kernel(*refs):
-    full_ref, prefix_ref = refs[-2:]
-    width = 128
-    for at in range(0, full_ref.shape[0], width):
-        prefix_ref[at : at + width, :] = unit_prefix(full_ref[at : at + width, :].astype(jnp.float32))
-
-
-def prefixes(after, full):
-    return pl.pallas_call(
-        prefix_kernel,
-        out_shape=jax.ShapeDtypeStruct((full.shape[0], PREFIX), jnp.bfloat16),
-        in_specs=[ANY] * len(after) + [VMEM],
-        out_specs=VMEM,
-        compiler_params=params(),
-        cost_estimate=pl.CostEstimate(flops=full.size * 8, bytes_accessed=4 << 20, transcendentals=0),
-    )(*after, full)
-
-
-def maxima(tokens_ref, queries, best_ref, count, width):
+def maxima(tokens_ref, queries, best_ref, count, width, prefix_ref=None):
     rows = queries.shape[0]
     for at in range(0, rows, 256):
         block = queries[at : at + 256, :]
         step = block.shape[0]
         for p in range(0, count, 2):
+            tokens = (tokens_ref if prefix_ref is None or at == 0 else prefix_ref)[p * width : (p + 2) * width, :]
+            if prefix_ref is not None and at == 0:
+                tokens = unit_prefix(tokens.astype(jnp.float32))
+                prefix_ref[p * width : (p + 2) * width, :] = tokens
             scores = lax.dot_general(
-                tokens_ref[p * width : (p + 2) * width, :],
+                tokens,
                 block,
                 (((1,), (1,)), ((), ())),
                 preferred_element_type=jnp.float32,
@@ -130,32 +116,42 @@
     out_ref[...] = average(best_ref, 0, places, places)
 
 
-def coarse_kernel(order, first, places, after_ref, tokens_ref, queries_ref, *rest):
-    out_ref, best_ref = rest[-2:]
-    count, width = best_ref.shape[0], tokens_ref.shape[0] // best_ref.shape[0]
-    maxima(tokens_ref, unit_prefix(queries_ref[...].astype(jnp.float32)), best_ref, count, width)
-
+def coarse(order, first, places, tokens_ref, queries_ref, best_ref, owners, *prefix):
     def whose(place):
         return regroup(place, order) ^ lax.axis_index("slab")
 
-    result = average(best_ref, first, places, out_ref.shape[0], whose)
-    out_ref[...] = result if len(rest) == 2 else rest[0][...] + result
-
-
-def score(kernel, rows, count, tokens, queries, after=(), partial=()):
+    count, width = best_ref.shape[0], tokens_ref.shape[0] // best_ref.shape[0]
+    maxima(tokens_ref, unit_prefix(queries_ref[...].astype(jnp.float32)), best_ref, count, width, *prefix)
+    return average(best_ref, first, places, owners, whose)
+
+
+def near_coarse_kernel(order, places, *refs):
+    full_ref, queries_ref, out_ref, prefix_ref, best_ref = refs[-5:]
+    out_ref[...] = coarse(order, 0, places, full_ref, queries_ref, best_ref, out_ref.shape[0], prefix_ref)
+
+
+def far_coarse_kernel(order, first, places, tokens_ref, queries_ref, partial_ref, out_ref, best_ref):
+    out_ref[...] = partial_ref[...] + coarse(order, first, places, tokens_ref, queries_ref, best_ref, out_ref.shape[0])
+
+
+def score(kernel, rows, count, tokens, queries, after=(), partial=(), prefix=False):
     places, qtok, dim = queries.shape
     queries = queries.reshape(places * qtok, dim)
-    return pl.pallas_call(
+    shapes = [jax.ShapeDtypeStruct((rows, count), jnp.float32)]
+    if prefix:
+        shapes.append(jax.ShapeDtypeStruct((tokens.shape[0], PREFIX), tokens.dtype))
+    found = pl.pallas_call(
         kernel,
-        out_shape=jax.ShapeDtypeStruct((rows, count), jnp.float32),
+        out_shape=shapes,
         in_specs=[ANY] * len(after) + [VMEM] * (2 + len(partial)),
-        out_specs=VMEM,
+        out_specs=[VMEM] * len(shapes),
         scratch_shapes=[pltpu.VMEM((count, places * qtok), jnp.float32)],
         compiler_params=params(),
         cost_estimate=pl.CostEstimate(
             flops=4 * tokens.shape[0] * places * qtok * 128, bytes_accessed=4 << 20, transcendentals=0
         ),
     )(*after, tokens, queries, *partial)
+    return found if prefix else found[0]
 
 
 def pick_kernel(count, order, coarse_ref, ids_ref, returned_ref, exact_out, coarse_out, picked_ref, sems):
@@ -224,30 +220,29 @@
     scores = [score(exact_kernel, half, count, full, join(*parts[: size // 2]))]
     for part in parts[size // 2 :]:
         scores.append(score(exact_kernel, part.shape[0], count, full, part))
-    coarse = None
+    result = None
     rows = join(*scores)
     for low, size in reversed(order):
         group = rows.shape[0] // size
         away = [exchange(rows[group * k : group * (k + 1)], low * k, owners) for k in reversed(range(1, size))]
         rows = jnp.concatenate([rows[:group]] + away[::-1], axis=1)
-        if coarse is None:
-            prefix = prefixes(scores, full)
-            near_kernel = functools.partial(coarse_kernel, order, 0, held.shape[0])
-            far_kernel = functools.partial(coarse_kernel, order, held.shape[0], owners - held.shape[0])
-            coarse = score(near_kernel, owners, count, prefix, held, after=(scores[-1],))
-            coarse = score(far_kernel, owners, count, prefix, join(*came), after=(scores[-1],), partial=(coarse,))
-    exact, coarse = pl.pallas_call(
+        if result is None:
+            near_kernel = functools.partial(near_coarse_kernel, order, held.shape[0])
+            far_kernel = functools.partial(far_coarse_kernel, order, held.shape[0], owners - held.shape[0])
+            result, prefix = score(near_kernel, owners, count, full, held, after=scores, prefix=True)
+            result = score(far_kernel, owners, count, prefix, join(*came), partial=(result,))
+    exact, result = pl.pallas_call(
         functools.partial(pick_kernel, count, order),
         out_shape=(
             jax.ShapeDtypeStruct(shortlist.shape, jnp.float32),
-            jax.ShapeDtypeStruct(coarse.shape, jnp.float32),
+            jax.ShapeDtypeStruct(result.shape, jnp.float32),
         ),
         in_specs=[VMEM, VMEM, VMEM],
         out_specs=(ANY, ANY),
         scratch_shapes=[pltpu.VMEM(shortlist.shape, jnp.float32), pltpu.SemaphoreType.DMA((2,))],
         compiler_params=params(),
-    )(coarse, shortlist, rows)
-    return (coarse.T, exact)
+    )(result, shortlist, rows)
+    return (result.T, exact)
 
 
 def solution(mesh):

time: 28.6 us -> 28.2 us (0.986)
  Pallas kernels: 9.61 us -> 9.02 us
  waiting for transfers between devices: 2.24 us -> 2.75 us
  starting transfers between devices: 14.3 us -> 13.9 us
    pallas_call x6 -> x5, Pallas kernels: 7.25 us -> 6.66 us  [score(): pl.pallas_call(kernel, out_shape=shapes, in_specs=[ANY] * len(after) + [V...]
    ppermute x12, waiting for transfers between devices: 2.24 us -> 2.75 us  [exchange(): return lax.ppermute(array, 'slab', [(i, i ^ offset) for i in range(owners)])]
    ppermute x12, starting transfers between devices: 14.3 us -> 13.9 us  [exchange(): return lax.ppermute(array, 'slab', [(i, i ^ offset) for i in range(owners)])]
    unnamed x8 -> x7, local copies, waits for them, and re-layouts: 1.42 us -> 1.41 us
  transfers between devices with their start and end apart: 12 -> 12, of which waited for: 2 -> 4; matrix products, arithmetic and copies ran while one was open for 3% -> 3% of each run, Pallas kernels for 28% -> 27%
where the time goes in v7:
time: 28.2 us; the launch traced here: 27.9 us
  starting transfers between devices  13.9 us (49%)
  Pallas kernels  9.02 us (32%)
  waiting for transfers between devices  2.75 us (10%)
  local copies, waits for them, and re-layouts  1.44 us (5%)
  between operations  0.7 us (2%)
    ppermute x12, starting transfers between devices, exchange(): return lax.ppermute(array, 'slab', [(i, i ^ offset) for i in range(owners)])  13.9 us
    pallas_call x5, Pallas kernels, score(): pl.pallas_call(kernel, out_shape=shapes, in_specs=[ANY] * len(after) + [V...  6.66 us
    ppermute x12, waiting for transfers between devices, exchange(): return lax.ppermute(array, 'slab', [(i, i ^ offset) for i in range(owners)])  2.75 us
    pallas_call x1, Pallas kernels, live_tokens(): pl.pallas_call(live_kernel, out_shape=jax.ShapeDtypeStruct((count * width...  1.64 us
    unnamed x7, local copies, waits for them, and re-layouts  1.41 us
    pallas_call x1, Pallas kernels, per_device(): pl.pallas_call(functools.partial(pick_kernel, count, order), out_shape=(j...  0.72 us
  transfers between devices with their start and end apart: 12, of which 4 were waited for; matrix products, arithmetic and copies ran while one was open for 3% of the time, Pallas kernels for 27%

profile of v7, /device:TPU:0, one launch (start us, length us, event | category | flops | bytes accessed | tf_op | source)
XLA Modules:
  0.0 27.9 jit_solution(5682372734265658402)
XLA Ops:
  0.6 4.1 %collective-permute-start = (bf16[1,32,128]{2,1,0:T(8,128)(2,1)}, bf16[1,32,128]{2,1,0:T(8,128)(2,1)S(1)}, u32[]{:S(2)}, u32[]{:S(2)}) collective-permute-start(bf16[1,32,128]{2,1,0:T(8,128)(2,1)} %param.4), channel_id=1, source_target_pairs={{0,8},{1,9},{2,10},{3,11},{4,12},{5,13},{6,14},{7,15},{8,0},{9,1},... | collective-permute-start | bytes 24584 | tf_op jit(solution)/shard_map/ppermute | solution.py:189
  4.7 1.3 %collective-permute-start.1 = (bf16[1,32,128]{2,1,0:T(8,128)(2,1)}, bf16[1,32,128]{2,1,0:T(8,128)(2,1)S(1)}, u32[]{:S(2)}, u32[]{:S(2)}) collective-permute-start(bf16[1,32,128]{2,1,0:T(8,128)(2,1)} %param.4), channel_id=1, source_target_pairs={{0,12},{1,13},{2,14},{3,15},{4,8},{5,9},{6,10},{7,11},{8,4},{9,5},... | collective-permute-start | bytes 24584 | tf_op jit(solution)/shard_map/ppermute | solution.py:189
  6.1 0.2 collective-permute-start.2
  6.3 0.7 %constant_dynamic-update-slice_fusion.3 = (bf16[4,32,128]{2,1,0:T(8,128)(2,1)S(1)}, bf16[8,32,128]{2,1,0:T(8,128)(2,1)S(1)}) fusion(bf16[1,32,128]{2,1,0:T(8,128)(2,1)} %param.4), kind=kLoop, calls=%fused_computation.4 | loop fusion | bytes 24576
  7.0 0.7 %copy-done = s32[64]{0:T(128)S(1)} copy-done((s32[64]{0:T(128)S(1)}, s32[64]{0:T(128)}, u32[]{:S(2)}) %copy-start) | copy-done | bytes 280
  7.7 1.6 %shard_map.59.tokens_ref.refs_3_ = bf16[8192,128]{1,0:T(8,128)(2,1)S(1)} custom-call(s32[64]{0:T(128)S(1)} %copy-done, bf16[64,128,128]{2,1,0:T(8,128)(2,1)} %passages_hbm.1), custom_call_target="tpu_custom_call" | custom-call | flops 8388608 | bytes 6291456 | tf_op jit(solution)/shard_map/pallas_call | solution.py:50
  9.4 1.0 %collective-permute-done.1 = bf16[1,32,128]{2,1,0:T(8,128)(2,1)S(1)} collective-permute-done((bf16[1,32,128]{2,1,0:T(8,128)(2,1)}, bf16[1,32,128]{2,1,0:T(8,128)(2,1)S(1)}, u32[]{:S(2)}, u32[]{:S(2)}) %collective-permute-start.1) | collective-permute-done | bytes 8224 | tf_op jit(solution)/shard_map/ppermute | solution.py:189
  10.5 1.6 %collective-permute-start.4 = (bf16[4,32,128]{2,1,0:T(8,128)(2,1)S(1)}, bf16[4,32,128]{2,1,0:T(8,128)(2,1)S(1)}, u32[]{:S(2)}, u32[]{:S(2)}) collective-permute-start(bf16[4,32,128]{2,1,0:T(8,128)(2,1)S(1)} %get-tuple-element.16), channel_id=1, source_target_pairs={{0,2},{1,3},{2,0},{3,1},{4,6},{5,7},{6,4},{7,5},{8,10},{9,11},{10,... | collective-permute-start | bytes 98312 | tf_op jit(solution)/shard_map/ppermute | solution.py:189
  12.1 0.3 collective-permute-start.5
  12.4 1.4 %shard_map.60.refs_0_ = f32[8,64]{1,0:T(8,128)S(1)} custom-call(bf16[8192,128]{1,0:T(8,128)(2,1)S(1)} %shard_map.59.tokens_ref.refs_3_, bf16[256,128]{1,0:T(8,128)(2,1)S(1)} %bitcast.10), custom_call_target="tpu_custom_call" | custom-call | flops 1073741824 | bytes 4194304 | tf_op jit(solution)/shard_map/pallas_call | solution.py:143
  13.8 0.7 %collective-permute-done.4 = bf16[4,32,128]{2,1,0:T(8,128)(2,1)S(1)} collective-permute-done((bf16[4,32,128]{2,1,0:T(8,128)(2,1)S(1)}, bf16[4,32,128]{2,1,0:T(8,128)(2,1)S(1)}, u32[]{:S(2)}, u32[]{:S(2)}) %collective-permute-start.4) | collective-permute-done | bytes 32800 | tf_op jit(solution)/shard_map/ppermute | solution.py:189
  14.5 0.8 %shard_map.61.refs_1_ = f32[4,64]{1,0:T(4,128)S(1)} custom-call(bf16[8192,128]{1,0:T(8,128)(2,1)S(1)} %shard_map.59.tokens_ref.refs_3_, bf16[128,128]{1,0:T(8,128)(2,1)S(1)} %bitcast.6), custom_call_target="tpu_custom_call" | custom-call | flops 536870912 | bytes 4194304 | tf_op jit(solution)/shard_map/pallas_call | solution.py:143
  15.3 0.1 collective-permute-done.5
  15.4 0.8 %shard_map.62.refs_2_ = f32[4,64]{1,0:T(4,128)S(1)} custom-call(bf16[8192,128]{1,0:T(8,128)(2,1)S(1)} %shard_map.59.tokens_ref.refs_3_, bf16[128,128]{1,0:T(8,128)(2,1)S(1)} %bitcast.7), custom_call_target="tpu_custom_call" | custom-call | flops 536870912 | bytes 4194304 | tf_op jit(solution)/shard_map/pallas_call | solution.py:143
  16.3 0.7 %collective-permute-start.8 = (f32[4,64]{1,0:T(4,128)S(1)}, f32[4,64]{1,0:T(4,128)S(1)}, u32[]{:S(2)}, u32[]{:S(2)}) collective-permute-start(f32[4,64]{1,0:T(4,128)S(1)} %shard_map.62.refs_2_), channel_id=1, source_target_pairs={{0,3},{1,2},{2,1},{3,0},{4,7},{5,6},{6,5},{7,4},{8,11},{9,10},{10,... | collective-permute-start | bytes 3080 | tf_op jit(solution)/shard_map/ppermute | solution.py:189
  17.0 1.1 %collective-permute-start.7 = (f32[4,64]{1,0:T(4,128)S(1)}, f32[4,64]{1,0:T(4,128)S(1)}, u32[]{:S(2)}, u32[]{:S(2)}) collective-permute-start(f32[4,64]{1,0:T(4,128)S(1)} %shard_map.61.refs_1_), channel_id=1, source_target_pairs={{0,2},{1,3},{2,0},{3,1},{4,6},{5,7},{6,4},{7,5},{8,10},{9,11},{10,... | collective-permute-start | bytes 3080 | tf_op jit(solution)/shard_map/ppermute | solution.py:189
  18.1 0.1 collective-permute-start.6
  18.2 1.6 %shard_map.63 = (f32[16,64]{1,0:T(8,128)S(1)}, bf16[8192,64]{1,0:T(8,128)(2,1)S(1)}) custom-call(f32[8,64]{1,0:T(8,128)S(1)} %shard_map.60.refs_0_, f32[4,64]{1,0:T(4,128)S(1)} %shard_map.61.refs_1_, f32[4,64]{1,0:T(4,128)S(1)} %shard_map.62.refs_2_, bf16[8192,128]{1,0:T(8,128)(2,1)S(1)} %shard_map.59.tokens_ref.refs_3_, bf16[128,128]{1,0:T(8,128)(2,1)S(1)} %bitcast.9), custom_call_target="tpu_custom_call" | custom-call | flops 536870912 | bytes 4194304 | tf_op jit(solution)/shard_map/pallas_call | solution.py:143
  19.8 0.8 %collective-permute-done.7 = f32[4,64]{1,0:T(4,128)S(1)} collective-permute-done((f32[4,64]{1,0:T(4,128)S(1)}, f32[4,64]{1,0:T(4,128)S(1)}, u32[]{:S(2)}, u32[]{:S(2)}) %collective-permute-start.7) | collective-permute-done | bytes 1056 | tf_op jit(solution)/shard_map/ppermute | solution.py:189
  20.7 2.0 %collective-permute-start.11 = (f32[1,256]{1,0:T(1,128)S(1)}, f32[1,256]{1,0:T(1,128)S(1)}, u32[]{:S(2)}, u32[]{:S(2)}) collective-permute-start(f32[1,256]{1,0:T(1,128)S(1)} %get-tuple-element.25), channel_id=1, source_target_pairs={{0,12},{1,13},{2,14},{3,15},{4,8},{5,9},{6,10},{7,11},{8,4},{9,5},... | collective-permute-start | bytes 3080 | tf_op jit(solution)/shard_map/ppermute | solution.py:189
  22.7 0.2 collective-permute-start.10
  23.0 2.1 %collective-permute-start.9 = (f32[1,256]{1,0:T(1,128)S(1)}, f32[1,256]{1,0:T(1,128)S(1)}, u32[]{:S(2)}, u32[]{:S(2)}) collective-permute-start(f32[1,256]{1,0:T(1,128)S(1)} %get-tuple-element.27), channel_id=1, source_target_pairs={{0,4},{1,5},{2,6},{3,7},{4,0},{5,1},{6,2},{7,3},{8,12},{9,13},{10,... | collective-permute-start | bytes 3080 | tf_op jit(solution)/shard_map/ppermute | solution.py:189
  25.1 2.0 %shard_map.64.coarse_ref = f32[16,64]{1,0:T(8,128)S(1)} custom-call(bf16[8192,64]{1,0:T(8,128)(2,1)S(1)} %get-tuple-element.12.tokens_ref, bf16[384,128]{1,0:T(8,128)(2,1)S(1)} %bitcast.8, f32[16,64]{1,0:T(8,128)S(1)} %get-tuple-element.13.partial_ref), custom_call_target="tpu_custom_call" | custom-call | flops 1610612736 | bytes 4194304 | tf_op jit(solution)/shard_map/pallas_call | solution.py:143
  27.2 0.7 %shard_map.65 = (f32[1,96]{1,0:T(1,128)}, f32[16,64]{1,0:T(8,128)}) custom-call(f32[16,64]{1,0:T(8,128)S(1)} %shard_map.64.coarse_ref, s32[1,96]{1,0:T(1,128)S(1)} %copy-done.1, f32[1,1024]{1,0:T(1,128)S(1)} %pad_maximum_fusion.2.returned_ref), custom_call_target="tpu_custom_call" | custom-call | tf_op jit(solution)/shard_map/pallas_call | solution.py:234
  (21 shorter events, 0.3 us)
Async XLA Ops:
  0.6 8.7 %collective-permute-start = (bf16[1,32,128]{2,1,0:T(8,128)(2,1)}, bf16[1,32,128]{2,1,0:T(8,128)(2,1)S(1)}, u32[]{:S(2)}, u32[]{:S(2)}) collective-permute-start(bf16[1,32,128]{2,1,0:T(8,128)(2,1)} %param.4), channel_id=1, source_target_pairs={{0,8},{1,9},{2,10},{3,11},{4,12},{5,13},{6,14},{7,15},{8,0},{9,1},... | collective-permute-start | bytes 24584 | tf_op jit(solution)/shard_map/ppermute | solution.py:189
  4.7 5.7 %collective-permute-start.1 = (bf16[1,32,128]{2,1,0:T(8,128)(2,1)}, bf16[1,32,128]{2,1,0:T(8,128)(2,1)S(1)}, u32[]{:S(2)}, u32[]{:S(2)}) collective-permute-start(bf16[1,32,128]{2,1,0:T(8,128)(2,1)} %param.4), channel_id=1, source_target_pairs={{0,12},{1,13},{2,14},{3,15},{4,8},{5,9},{6,10},{7,11},{8,4},{9,5},... | collective-permute-start | bytes 24584 | tf_op jit(solution)/shard_map/ppermute | solution.py:189
  6.1 4.3 %collective-permute-start.2 = (bf16[1,32,128]{2,1,0:T(8,128)(2,1)}, bf16[1,32,128]{2,1,0:T(8,128)(2,1)S(1)}, u32[]{:S(2)}, u32[]{:S(2)}) collective-permute-start(bf16[1,32,128]{2,1,0:T(8,128)(2,1)} %param.4), channel_id=1, source_target_pairs={{0,4},{1,5},{2,6},{3,7},{4,0},{5,1},{6,2},{7,3},{8,12},{9,13},{10,... | collective-permute-start | bytes 24584 | tf_op jit(solution)/shard_map/ppermute | solution.py:189
  7.0 0.7 %copy-start = (s32[64]{0:T(128)S(1)}, s32[64]{0:T(128)}, u32[]{:S(2)}) copy-start(s32[64]{0:T(128)} %lens_hbm.1) | copy-start | bytes 772
  10.4 1.9 %collective-permute-start.3 = (bf16[4,32,128]{2,1,0:T(8,128)(2,1)S(1)}, bf16[4,32,128]{2,1,0:T(8,128)(2,1)S(1)}, u32[]{:S(2)}, u32[]{:S(2)}) collective-permute-start(bf16[4,32,128]{2,1,0:T(8,128)(2,1)S(1)} %get-tuple-element.16), channel_id=1, source_target_pairs={{0,1},{1,0},{2,3},{3,2},{4,5},{5,4},{6,7},{7,6},{8,9},{9,8},{10,11... | collective-permute-start | bytes 98312 | tf_op jit(solution)/shard_map/ppermute | solution.py:189
  10.5 4.0 %collective-permute-start.4 = (bf16[4,32,128]{2,1,0:T(8,128)(2,1)S(1)}, bf16[4,32,128]{2,1,0:T(8,128)(2,1)S(1)}, u32[]{:S(2)}, u32[]{:S(2)}) collective-permute-start(bf16[4,32,128]{2,1,0:T(8,128)(2,1)S(1)} %get-tuple-element.16), channel_id=1, source_target_pairs={{0,2},{1,3},{2,0},{3,1},{4,6},{5,7},{6,4},{7,5},{8,10},{9,11},{10,... | collective-permute-start | bytes 98312 | tf_op jit(solution)/shard_map/ppermute | solution.py:189
  12.1 3.3 %collective-permute-start.5 = (bf16[4,32,128]{2,1,0:T(8,128)(2,1)S(1)}, bf16[4,32,128]{2,1,0:T(8,128)(2,1)S(1)}, u32[]{:S(2)}, u32[]{:S(2)}) collective-permute-start(bf16[4,32,128]{2,1,0:T(8,128)(2,1)S(1)} %get-tuple-element.16), channel_id=1, source_target_pairs={{0,3},{1,2},{2,1},{3,0},{4,7},{5,6},{6,5},{7,4},{8,11},{9,10},{10,... | collective-permute-start | bytes 98312 | tf_op jit(solution)/shard_map/ppermute | solution.py:189
  16.3 3.5 %collective-permute-start.8 = (f32[4,64]{1,0:T(4,128)S(1)}, f32[4,64]{1,0:T(4,128)S(1)}, u32[]{:S(2)}, u32[]{:S(2)}) collective-permute-start(f32[4,64]{1,0:T(4,128)S(1)} %shard_map.62.refs_2_), channel_id=1, source_target_pairs={{0,3},{1,2},{2,1},{3,0},{4,7},{5,6},{6,5},{7,4},{8,11},{9,10},{10,... | collective-permute-start | bytes 3080 | tf_op jit(solution)/shard_map/ppermute | solution.py:189
  17.0 3.6 %collective-permute-start.7 = (f32[4,64]{1,0:T(4,128)S(1)}, f32[4,64]{1,0:T(4,128)S(1)}, u32[]{:S(2)}, u32[]{:S(2)}) collective-permute-start(f32[4,64]{1,0:T(4,128)S(1)} %shard_map.61.refs_1_), channel_id=1, source_target_pairs={{0,2},{1,3},{2,0},{3,1},{4,6},{5,7},{6,4},{7,5},{8,10},{9,11},{10,... | collective-permute-start | bytes 3080 | tf_op jit(solution)/shard_map/ppermute | solution.py:189
  18.1 2.5 %collective-permute-start.6 = (f32[4,64]{1,0:T(4,128)S(1)}, f32[4,64]{1,0:T(4,128)S(1)}, u32[]{:S(2)}, u32[]{:S(2)}) collective-permute-start(f32[4,64]{1,0:T(4,128)S(1)} %get-tuple-element.29), channel_id=1, source_target_pairs={{0,1},{1,0},{2,3},{3,2},{4,5},{5,4},{6,7},{7,6},{8,9},{9,8},{10,11... | collective-permute-start | bytes 3080 | tf_op jit(solution)/shard_map/ppermute | solution.py:189
  20.7 6.5 %collective-permute-start.11 = (f32[1,256]{1,0:T(1,128)S(1)}, f32[1,256]{1,0:T(1,128)S(1)}, u32[]{:S(2)}, u32[]{:S(2)}) collective-permute-start(f32[1,256]{1,0:T(1,128)S(1)} %get-tuple-element.25), channel_id=1, source_target_pairs={{0,12},{1,13},{2,14},{3,15},{4,8},{5,9},{6,10},{7,11},{8,4},{9,5},... | collective-permute-start | bytes 3080 | tf_op jit(solution)/shard_map/ppermute | solution.py:189
  22.7 4.5 %collective-permute-start.10 = (f32[1,256]{1,0:T(1,128)S(1)}, f32[1,256]{1,0:T(1,128)S(1)}, u32[]{:S(2)}, u32[]{:S(2)}) collective-permute-start(f32[1,256]{1,0:T(1,128)S(1)} %get-tuple-element.26), channel_id=1, source_target_pairs={{0,8},{1,9},{2,10},{3,11},{4,12},{5,13},{6,14},{7,15},{8,0},{9,1},... | collective-permute-start | bytes 3080 | tf_op jit(solution)/shard_map/ppermute | solution.py:189
  23.0 4.2 %collective-permute-start.9 = (f32[1,256]{1,0:T(1,128)S(1)}, f32[1,256]{1,0:T(1,128)S(1)}, u32[]{:S(2)}, u32[]{:S(2)}) collective-permute-start(f32[1,256]{1,0:T(1,128)S(1)} %get-tuple-element.27), channel_id=1, source_target_pairs={{0,4},{1,5},{2,6},{3,7},{4,0},{5,1},{6,2},{7,3},{8,12},{9,13},{10,... | collective-permute-start | bytes 3080 | tf_op jit(solution)/shard_map/ppermute | solution.py:189
  25.1 2.1 %copy-start.1 = (s32[1,96]{1,0:T(1,128)S(1)}, s32[1,96]{1,0:T(1,128)}, u32[]{:S(2)}) copy-start(s32[1,96]{1,0:T(1,128)} %ids_ref.1) | copy-start | bytes 1156
